TPU v7x, 32 devices: a whole 2x2x4 slice. The times are simulated.
32 devices in a mesh: grp: 4 (over x, core), rep: 8 (over z, y).
Axes of the slice: x: 2, y: 2, z: 4, core: 2. Of those that a mesh axis runs over, the one named last changes fastest.
Arguments:
- features: bfloat16 [16384, 768], P(('grp', 'rep')), may hold values from -6 to 6
- fetch_row: int32 [16, 512], P('grp', 'rep'), may hold values from 0 to 511
- live_count: int32 [16, 8], P('grp', 'rep'), may hold values from 16 to 64, as said below
- seed_features: bfloat16 [16384, 768], P(('grp', 'rep')), may hold values from -6 to 6
- tile_block: int32 [128, 2], P(('grp', 'rep')), may hold values from 0 to 1, each once within a row
- tile_weight: bfloat16 [128, 2, 128, 128], P(('grp', 'rep')), may hold values from -0.375 to 0.375
- self_weight: bfloat16 [768, 512], replicated, may hold values from -0.21875 to 0.21875
- neighbour_weight: bfloat16 [768, 512], replicated, may hold values from -0.21875 to 0.21875
- layer_bias: float32 [512], replicated, may hold values from -4 to 4
- cotangent: bfloat16 [16384, 512], P(('grp', 'rep')), may hold values from -6 to 6
Outputs:
- weight_grad: float32 [512, 768], P('grp', 'rep')
Inputs may be any that keep to these rules, and one draw needn't show every extreme that they name: `live_count`: slots at or past the count are padding. In every draw, for each rep index some owner is asked for all 64 slots by every device of its group. `tile_block`: each row names every block of a device's fetched rows once.
All inputs are finite; a program needn't handle non-finite values.
Results may differ from a plain program's by a relative error of at most 0.0043.
Values may be sent and summed in bfloat16 or wider, within the bound.
A program may use at most 64 MiB of HBM per device.

v0:
```python
import jax
import jax.numpy as jnp
from jax import lax
from jax.sharding import PartitionSpec as P


def body(
    features,
    fetch_row,
    live_count,
    seed_features,
    tile_block,
    tile_weight,
    self_weight,
    neighbour_weight,
    layer_bias,
    cotangent,
):
    width = features.shape[1]
    asked = lax.all_to_all(fetch_row, "grp", split_axis=0, concat_axis=0, tiled=True)
    table_rows = jnp.take(features, asked.reshape(-1), axis=0).reshape(asked.shape + (width,))
    fetched = lax.all_to_all(table_rows, "grp", split_axis=0, concat_axis=0, tiled=True)
    live_mask = lax.broadcasted_iota(jnp.int32, fetch_row.shape, 1) < live_count
    fetched = jnp.where(live_mask[:, :, None], fetched, jnp.zeros((), fetched.dtype))
    row_blocks = fetched.reshape(-1, 128, width)
    chosen = jnp.take(row_blocks, tile_block, axis=0)
    aggregated = jnp.einsum(
        "bkij,bkjf->bif", tile_weight, chosen, preferred_element_type=jnp.float32
    )
    aggregated = aggregated.reshape(-1, width).astype(jnp.bfloat16)
    pre_act = jnp.dot(seed_features, self_weight, preferred_element_type=jnp.float32)
    pre_act = pre_act + jnp.dot(aggregated, neighbour_weight, preferred_element_type=jnp.float32)
    pre_act = pre_act + layer_bias[None, :]
    sigmoid_val = jax.nn.sigmoid(pre_act)
    slope = sigmoid_val * (1.0 + pre_act * (1.0 - sigmoid_val))
    grad_pre = (cotangent.astype(jnp.float32) * slope).astype(jnp.bfloat16)
    partial_sum = lax.psum_scatter(
        lax.dot_general(
            grad_pre, aggregated, (((0,), (0,)), ((), ())), preferred_element_type=jnp.float32
        ),
        "grp",
        scatter_dimension=0,
        tiled=True,
    )
    return lax.psum_scatter(partial_sum, "rep", scatter_dimension=1, tiled=True)


def solution(mesh):
    placed = (
        P(("grp", "rep"), None),
        P("grp", "rep"),
        P("grp", "rep"),
        P(("grp", "rep"), None),
        P(("grp", "rep"), None),
        P(("grp", "rep"), None, None, None),
        P(),
        P(),
        P(),
        P(("grp", "rep"), None),
    )
    return jax.shard_map(
        body, mesh=mesh, in_specs=placed, out_specs=P("grp", "rep"), check_vma=False
    )
```

profile of v0, /device:TPU:0, one launch (start us, length us, event | category | flops | bytes accessed | tf_op | source)
XLA Modules:
  0.0 138.6 jit_solution(2393882084800354953)
XLA Ops:
  6.5 4.3 %all-to-all-start = ((s32[4,1,64]{2,1,0:T(1,128)}), s32[4,1,64]{2,1,0:T(1,128)S(1)}, u32[]{:S(2)}, u32[]{:S(2)}) async-start(s32[4,1,64]{2,1,0:T(1,128)} %bitcast.27), calls=%async_computation | async-start | bytes 4096 | tf_op jit(solution)/shard_map/all_to_all | solution.py:20
  10.9 0.7 compare_select_fusion.2
  11.6 0.7 compare_and_fusion.1
  12.2 0.7 iota_compare_fusion
  13.0 0.1 copy.18
  13.1 0.1 reshape.94
  13.1 1.4 %all-to-all-done = s32[4,1,64]{2,1,0:T(1,128)S(1)} async-done(((s32[4,1,64]{2,1,0:T(1,128)}), s32[4,1,64]{2,1,0:T(1,128)S(1)}, u32[]{:S(2)}, u32[]{:S(2)}) %all-to-all-start) | async-done | bytes 1056 | tf_op jit(solution)/shard_map/all_to_all | solution.py:20
  14.6 0.5 broadcast.74
  15.1 0.7 reduce.3
  15.7 0.1 reshape.82
  15.8 2.6 %gather_fusion = bf16[256,768]{1,0:T(8,128)(2,1)S(1)} fusion(bf16[512,768]{1,0:T(8,128)(2,1)} %param.10, s32[1024]{0:T(1024)S(1)} %pad_clamp_fusion.1), kind=kCustom, calls=%fused_computation | custom fusion | bytes 787456 | tf_op jit(solution)/shard_map/jit(_take)/gather | solution.py:21
  18.5 0.9 broadcast_select_fusion
  19.4 3.5 %all-to-all-start.1 = ((bf16[4,64,768]{2,1,0:T(8,128)(2,1)}), bf16[4,64,768]{2,1,0:T(8,128)(2,1)S(1)}, u32[]{:S(2)}, u32[]{:S(2)}) async-start(bf16[4,64,768]{2,1,0:T(8,128)(2,1)} %broadcast_select_fusion), calls=%async_computation.1 | async-start | bytes 786432 | tf_op jit(solution)/shard_map/all_to_all | solution.py:22
  22.9 0.1 copy.17
  23.0 1.5 %fusion.13 = f32[512,512]{1,0:T(8,128)} fusion(bf16[512,768]{1,0:T(8,128)(2,1)S(1)} %copy-done.2, bf16[768,512]{1,0:T(8,128)(2,1)S(1)} %copy-done.3), kind=kOutput, calls=%fused_computation.26 | convolution fusion | flops 402653184 | bytes 2621440 | tf_op jit(solution)/shard_map/dot_general | solution.py:31
  24.6 5.7 %all-to-all-done.1 = bf16[4,64,768]{2,1,0:T(8,128)(2,1)S(1)} async-done(((bf16[4,64,768]{2,1,0:T(8,128)(2,1)}), bf16[4,64,768]{2,1,0:T(8,128)(2,1)S(1)}, u32[]{:S(2)}, u32[]{:S(2)}) %all-to-all-start.1) | async-done | bytes 393248 | tf_op jit(solution)/shard_map/all_to_all | solution.py:22
  30.2 0.1 broadcast_select_fusion.1
  30.4 0.6 gather_fusion.1
  31.0 2.5 %bitcast_convert_fusion = bf16[4,768,128]{1,2,0:T(8,128)(2,1)} fusion(bf16[4,2,128,128]{3,2,1,0:T(8,128)(2,1)} %param.15, bf16[4,2,128,768]{3,2,1,0:T(8,128)(2,1)S(1)} %bitcast.23, pred[4,2]{1,0:T(4,128)(4,1)S(1)} %copy.17), kind=kOutput, calls=%fused_computation.2 | convolution fusion | flops 202506240 | bytes 2621448 | tf_op jit(solution)/shard_map/bkij,bkjf->bif/dot_general | solution.py:27
  33.5 4.1 %fusion.6 = f32[512,768]{1,0:T(8,128)} fusion(bf16[512,768]{1,0:T(8,128)(2,1)} %bitcast.29, f32[512,512]{1,0:T(8,128)S(1)} %copy-done.1, bf16[768,512]{1,0:T(8,128)(2,1)S(1)} %copy-done, bf16[512,512]{1,0:T(8,128)(2,1)} %param.19, f32[512]{0:T(512)S(1)} %copy-done.4), kind=kOutput, calls=%fused_computation.9 | convolution fusion | flops 808452096 | bytes 4720640 | tf_op jit(solution)/shard_map/dot_general | solution.py:38
  37.6 0.0 reduce-scatter.7.cloned.1.call-start
  37.6 29.0 %reduce-scatter.5.cloned.1.call-done = f32[128,768]{1,0:T(8,128)} async-done(((f32[512,768]{1,0:T(8,128)}), f32[128,768]{1,0:T(8,128)}) %reduce-scatter.5.cloned.1.call-update) | async-done | bytes 393232 | tf_op jit(solution)/shard_map/reduce_scatter | solution.py:37
  66.7 1.9 %copy.21 = f32[128,768]{0,1:T(8,128)} copy(f32[128,768]{1,0:T(8,128)} %reduce-scatter.5.cloned.1.call-done) | data formatting | bytes 786432
  68.6 63.2 %reduce-scatter.7.cloned.1.call-done = f32[96,128]{1,0:T(8,128)} async-done(((f32[768,128]{1,0:T(8,128)}), f32[96,128]{1,0:T(8,128)}) %reduce-scatter.7.cloned.1.call-update) | async-done | bytes 49168
  (17 shorter events, 0.1 us)
Async XLA Ops:
  6.5 27.0 %copy-start = (bf16[768,512]{1,0:T(8,128)(2,1)S(1)}, bf16[768,512]{1,0:T(8,128)(2,1)}, u32[]{:S(2)}) copy-start(bf16[768,512]{1,0:T(8,128)(2,1)} %param.17) | copy-start | bytes 2359300
  6.5 8.0 %all-to-all-start = ((s32[4,1,64]{2,1,0:T(1,128)}), s32[4,1,64]{2,1,0:T(1,128)S(1)}, u32[]{:S(2)}, u32[]{:S(2)}) async-start(s32[4,1,64]{2,1,0:T(1,128)} %bitcast.27), calls=%async_computation | async-start | bytes 4096 | tf_op jit(solution)/shard_map/all_to_all | solution.py:20
  18.5 4.5 %copy-start.2 = (bf16[512,768]{1,0:T(8,128)(2,1)S(1)}, bf16[512,768]{1,0:T(8,128)(2,1)}, u32[]{:S(2)}) copy-start(bf16[512,768]{1,0:T(8,128)(2,1)} %param.13) | copy-start | bytes 2359300
  18.5 4.5 %copy-start.3 = (bf16[768,512]{1,0:T(8,128)(2,1)S(1)}, bf16[768,512]{1,0:T(8,128)(2,1)}, u32[]{:S(2)}) copy-start(bf16[768,512]{1,0:T(8,128)(2,1)} %param.16) | copy-start | bytes 2359300
  19.4 10.9 %all-to-all-start.1 = ((bf16[4,64,768]{2,1,0:T(8,128)(2,1)}), bf16[4,64,768]{2,1,0:T(8,128)(2,1)S(1)}, u32[]{:S(2)}, u32[]{:S(2)}) async-start(bf16[4,64,768]{2,1,0:T(8,128)(2,1)} %broadcast_select_fusion), calls=%async_computation.1 | async-start | bytes 786432 | tf_op jit(solution)/shard_map/all_to_all | solution.py:22
  22.8 43.8 %reduce-scatter.5.cloned.1.call-start = ((), (), s32[]{:S(2)}) async-start(), calls=%async_computation.4 | async-start | bytes 1966080 | tf_op jit(solution)/shard_map/reduce_scatter | solution.py:37
  31.0 2.5 %copy-start.1 = (f32[512,512]{1,0:T(8,128)S(1)}, f32[512,512]{1,0:T(8,128)}, u32[]{:S(2)}) copy-start(f32[512,512]{1,0:T(8,128)} %fusion.13) | copy-start | bytes 3145732
  31.0 2.5 %copy-start.4 = (f32[512]{0:T(512)S(1)}, f32[512]{0:T(512)}, u32[]{:S(2)}) copy-start(f32[512]{0:T(512)} %param.18) | copy-start | bytes 6148
  37.6 94.2 %reduce-scatter.7.cloned.1.call-start = ((), (), s32[]{:S(2)}) async-start(), calls=%async_computation.5 | async-start | bytes 442368
Sparse Core Ops, SparseCore 0:
  37.7 28.8 reduce-scatter.4
  70.3 61.4 reduce-scatter.6
where the time goes:
time: 139 us
  waiting for transfers between devices  99.3 us (71%)
  between operations  13.5 us (10%)
  matrix products  8.06 us (6%)
  starting transfers between devices  7.88 us (6%)
  local copies, waits for them, and re-layouts  6.11 us (4%)
  other arithmetic  3.76 us (3%)
    unnamed x3, waiting for transfers between devices  63.2 us
    reduce_scatter x1, waiting for transfers between devices, body(): lax.psum_scatter(lax.dot_general(grad_pre, aggregated, (((0,), (0,)), (()...  29 us
    all_to_all x1, waiting for transfers between devices, body(): lax.all_to_all(table_rows, 'grp', split_axis=0, concat_axis=0, tiled=True)  5.68 us
    all_to_all x1, starting transfers between devices, body(): lax.all_to_all(fetch_row, 'grp', split_axis=0, concat_axis=0, tiled=True)  4.34 us
    dot_general x1, matrix products, body(): lax.dot_general(grad_pre, aggregated, (((0,), (0,)), ((), ())), preferred...  4.06 us
    all_to_all x1, starting transfers between devices, body(): lax.all_to_all(table_rows, 'grp', split_axis=0, concat_axis=0, tiled=True)  3.46 us
  transfers between devices with their start and end apart: 4, of which 4 were waited for; matrix products, arithmetic and copies ran while one was open for 3% of the time, Pallas kernels for 0%

commit v1 on v0

--- a/solution.py
+++ b/solution.py
@@ -1,10 +1,255 @@
+import functools
+
 import jax
 import jax.numpy as jnp
 from jax import lax
+from jax.experimental import pallas as pl
+from jax.experimental.pallas import tpu as pltpu
 from jax.sharding import PartitionSpec as P
 
-
-def body(
+MESH = pl.DeviceIdType.MESH
+BF16 = jnp.bfloat16
+F32 = jnp.float32
+
+
+def dot(a, b, ca=1, cb=0):
+    return lax.dot_general(a, b, (((ca,), (cb,)), ((), ())), preferred_element_type=F32)
+
+
+def kernel(
+    feat_hbm, row_hbm, live_hbm, seed_hbm, block_hbm, tile_hbm, self_hbm, neigh_hbm, bias_hbm, cot_hbm,
+    out_ref,
+    feat, row, live, seeds, block, tile, w_self, w_neigh, bias, cot,
+    request, asked, table_rows, fetched, mixed, hidden,
+    send_c, recv_c, own, send_1, recv_1, send_2, recv_2, send_3, recv_3,
+    load_sem, ask_send, ask_recv, row_send, row_recv,
+    c_send, c_recv, s1_send, s1_recv, s2_send, s2_recv, s3_send, s3_recv,
+):
+    g, r = lax.axis_index("grp"), lax.axis_index("rep")
+    x, c = g // 2, g % 2
+    z, y = r // 2, r % 2
+    n_z = send_3.shape[0]
+    part = send_3.shape[2]
+    slots = row.shape[1]
+    sib, x_near, x_far = x * 2 + (1 - c), (1 - x) * 2 + c, (1 - x) * 2 + (1 - c)
+    group = (x_near, x_far, sib)
+    y_near = z * 2 + (1 - y)
+
+    def at(grp, rep):
+        return {"grp": grp, "rep": rep}
+
+    loads = []
+    for k, (src, dst) in enumerate((
+        (row_hbm, row), (live_hbm, live), (feat_hbm, feat), (seed_hbm, seeds), (self_hbm, w_self),
+        (block_hbm, block), (tile_hbm, tile), (neigh_hbm, w_neigh), (bias_hbm, bias), (cot_hbm, cot),
+    )):
+        load = pltpu.make_async_copy(src, dst, load_sem.at[k])
+        load.start()
+        loads.append(load)
+
+    barrier = pltpu.get_barrier_semaphore()
+    for peer in group:
+        pl.semaphore_signal(barrier, inc=1, device_id=at(peer, r), device_id_type=MESH)
+    pl.semaphore_signal(barrier, inc=1, device_id=at(g, y_near), device_id_type=MESH)
+    for d in range(1, n_z):
+        pl.semaphore_signal(barrier, inc=1, device_id=at(g, (z + d) % n_z * 2 + y), device_id_type=MESH)
+
+    loads[0].wait()
+    loads[1].wait()
+    slot_ix = lax.broadcasted_iota(jnp.int32, row.shape, 1)
+    wanted = jnp.where(slot_ix < live[...], row[...], -1)
+    for p in range(4):
+        line = jnp.broadcast_to(wanted[p : p + 1, :], (8, slots))
+        request[p, :, 0:slots] = line
+        request[p, :, slots : 2 * slots] = line
+    pl.semaphore_wait(barrier, 3 + n_z)
+
+    asks = []
+    for k, peer in enumerate(group):
+        copy = pltpu.make_async_remote_copy(
+            src_ref=request.at[peer], dst_ref=asked.at[g], send_sem=ask_send.at[k], recv_sem=ask_recv.at[k],
+            device_id=at(peer, r), device_id_type=MESH,
+        )
+        copy.start()
+        asks.append(copy)
+    asked[g] = request[g]
+    loads[2].wait()
+
+    def gather(chip):
+        lane = lax.broadcasted_iota(jnp.int32, (1, 2 * slots), 1)
+        ix = jnp.where(lane < slots, asked[2 * chip][0:1, :], asked[2 * chip + 1][0:1, :])
+        rows_ix = lax.broadcasted_iota(jnp.int32, (feat.shape[0], 2 * slots), 0)
+        pick = jnp.where(rows_ix == ix, 1.0, 0.0).astype(BF16)
+        rows = dot(pick, feat[...], 0, 0).astype(BF16)
+        table_rows[2 * chip] = rows[0:slots]
+        table_rows[2 * chip + 1] = rows[slots : 2 * slots]
+
+    def row_copy(k):
+        return pltpu.make_async_remote_copy(
+            src_ref=table_rows.at[group[k]], dst_ref=fetched.at[g], send_sem=row_send.at[k],
+            recv_sem=row_recv.at[k], device_id=at(group[k], r), device_id_type=MESH,
+        )
+
+    asks[0].wait()
+    asks[1].wait()
+    gather(1 - x)
+    rows_out = [row_copy(0), row_copy(1), row_copy(2)]
+    rows_out[0].start()
+    rows_out[1].start()
+    asks[2].wait()
+    gather(x)
+    rows_out[2].start()
+    fetched[g] = table_rows[g]
+
+    loads[3].wait()
+    loads[4].wait()
+    hidden[...] = dot(seeds[...], w_self[...])
+    for k in range(5, 10):
+        loads[k].wait()
+    n_b, n_k, rows_b, cols_b = tile.shape
+    order = block[...]
+    for b in range(n_b):
+        for j in range(n_k):
+            total = jnp.zeros((rows_b, cols_b), F32)
+            for k in range(n_k):
+                here = jnp.broadcast_to(order[b : b + 1, k : k + 1], (rows_b, cols_b)) == j
+                total = jnp.where(here, tile[b, k].astype(F32), total)
+            mixed[b * rows_b : (b + 1) * rows_b, j * cols_b : (j + 1) * cols_b] = total.astype(BF16)
+    hidden[...] += bias[...]
+    for copy in rows_out:
+        copy.wait()
+
+    rows_in = fetched[...].reshape(4 * slots, fetched.shape[2])
+    agg = dot(mixed[...], rows_in).astype(BF16)
+    pre = hidden[...] + dot(agg, w_neigh[...])
+    sig = 0.5 * jnp.tanh(0.5 * pre) + 0.5
+    grad = (cot[...].astype(F32) * (sig * (1.0 + pre * (1.0 - sig)))).astype(BF16)
+    lanes = own.shape[-1]
+
+    def half(core):
+        cols = [grad[:, (2 * k) * lanes : (2 * k + 1) * lanes] for k in range(2)]
+        cols_1 = [grad[:, (2 * k + 1) * lanes : (2 * k + 2) * lanes] for k in range(2)]
+        first, second = jnp.concatenate(cols, axis=1), jnp.concatenate(cols_1, axis=1)
+        return dot(agg, jnp.where(core == 0, first, second), 0, 0)
+
+    def scatter(ref, value, kind):
+        for rep in range(2 * n_z):
+            rz, ry = rep // 2, rep % 2
+            for h in range(2):
+                lo = rep * 2 * part + h * part
+                for rx in range(2):
+                    piece = value[lo : lo + part, rx * lanes : (rx + 1) * lanes].astype(kind)
+                    ref[(h,) + ((rx, ry) if h == 0 else (ry, rx)) + (rz,)] = piece
+
+    scatter(send_c, half(1 - c), BF16)
+    core_out = []
+    for h in range(2):
+        copy = pltpu.make_async_remote_copy(
+            src_ref=send_c.at[h], dst_ref=recv_c.at[h], send_sem=c_send.at[h], recv_sem=c_recv.at[h],
+            device_id=at(sib, r), device_id_type=MESH,
+        )
+        copy.start()
+        core_out.append(copy)
+    scatter(own, half(c), F32)
+
+    near = (at(x_near, r), at(g, y_near))
+    place = (x, y)
+    outs_1 = []
+    for h in range(2):
+        core_out[h].wait()
+        i = place[h]
+        send_1[h] = (own[h, 1 - i] + recv_c[h, 1 - i].astype(F32)).astype(BF16)
+        copy = pltpu.make_async_remote_copy(
+            src_ref=send_1.at[h], dst_ref=recv_1.at[h], send_sem=s1_send.at[h], recv_sem=s1_recv.at[h],
+            device_id=near[h], device_id_type=MESH,
+        )
+        copy.start()
+        outs_1.append(copy)
+    for h in range(2):
+        i = place[h]
+        own[h, i] = own[h, i] + recv_c[h, i].astype(F32)
+    outs_2 = []
+    for h in range(2):
+        outs_1[h].wait()
+        i, j = place[h], place[1 - h]
+        send_2[h] = (own[h, i, 1 - j] + recv_1[h, 1 - j].astype(F32)).astype(BF16)
+        copy = pltpu.make_async_remote_copy(
+            src_ref=send_2.at[h], dst_ref=recv_2.at[h], send_sem=s2_send.at[h], recv_sem=s2_recv.at[h],
+            device_id=near[1 - h], device_id_type=MESH,
+        )
+        copy.start()
+        outs_2.append(copy)
+    for h in range(2):
+        i, j = place[h], place[1 - h]
+        own[h, i, j] = own[h, i, j] + recv_1[h, j].astype(F32)
+    for h in range(2):
+        outs_2[h].wait()
+        i, j = place[h], place[1 - h]
+        done = own[h, i, j] + recv_2[h].astype(F32)
+        own[h, i, j] = done
+        for rz in range(n_z):
+            send_3[rz, h] = done[rz].astype(BF16)
+    outs_3 = []
+    for d in range(1, n_z):
+        to = (z + d) % n_z
+        copy = pltpu.make_async_remote_copy(
+            src_ref=send_3.at[to], dst_ref=recv_3.at[d - 1], send_sem=s3_send.at[d - 1],
+            recv_sem=s3_recv.at[d - 1], device_id=at(g, to * 2 + y), device_id_type=MESH,
+        )
+        copy.start()
+        outs_3.append(copy)
+    total = jnp.concatenate([own[h, place[h], place[1 - h], z] for h in range(2)], axis=0)
+    for copy in outs_3:
+        copy.wait()
+    for d in range(n_z - 1):
+        total = total + recv_3[d].astype(F32).reshape(total.shape)
+    out_ref[...] = total.T
+
+
+def fused(features, fetch_row, live_count, seed_features, tile_block, tile_weight, self_weight, neighbour_weight, layer_bias, cotangent):
+    width, hid = neighbour_weight.shape
+    seeds = seed_features.shape[0]
+    slots = fetch_row.shape[1]
+    n_z = 4
+    lanes = hid // 4
+    part = width // (4 * n_z)
+    bias = layer_bias.reshape(1, hid)
+    operands = (features, fetch_row, live_count, seed_features, tile_block, tile_weight, self_weight, neighbour_weight, bias, cotangent)
+    n_b, n_k, rows_b, cols_b = tile_weight.shape
+    vmem = pltpu.VMEM
+    dma = pltpu.SemaphoreType.DMA
+    return pl.pallas_call(
+        kernel,
+        out_shape=jax.ShapeDtypeStruct((lanes, width // (2 * n_z)), F32),
+        in_specs=[pl.BlockSpec(memory_space=pl.ANY)] * len(operands),
+        out_specs=pl.BlockSpec(memory_space=vmem),
+        scratch_shapes=[vmem(a.shape, a.dtype) for a in operands] + [
+            vmem((4, 8, 2 * slots), jnp.int32),
+            vmem((4, 8, 2 * slots), jnp.int32),
+            vmem((4, slots, width), BF16),
+            vmem((4, slots, width), BF16),
+            vmem((seeds, n_k * cols_b), BF16),
+            vmem((seeds, hid), F32),
+            vmem((2, 2, 2, n_z, part, lanes), BF16),
+            vmem((2, 2, 2, n_z, part, lanes), BF16),
+            vmem((2, 2, 2, n_z, part, lanes), F32),
+            vmem((2, 2, n_z, part, lanes), BF16),
+            vmem((2, 2, n_z, part, lanes), BF16),
+            vmem((2, n_z, part, lanes), BF16),
+            vmem((2, n_z, part, lanes), BF16),
+            vmem((n_z, 2, part, lanes), BF16),
+            vmem((n_z - 1, 2, part, lanes), BF16),
+            dma((10,)), dma((3,)), dma((3,)), dma((3,)), dma((3,)),
+            dma((2,)), dma((2,)), dma((2,)), dma((2,)), dma((2,)), dma((2,)), dma((n_z - 1,)), dma((n_z - 1,)),
+        ],
+        compiler_params=pltpu.CompilerParams(
+            collective_id=0, has_side_effects=True, vmem_limit_bytes=48 * 1024 * 1024
+        ),
+        name="sage_step",
+    )(*operands)
+
+
+def plain(
     features,
     fetch_row,
     live_count,
@@ -58,6 +303,7 @@
         P(),
         P(("grp", "rep"), None),
     )
+    body = fused if (mesh.shape["grp"], mesh.shape["rep"]) == (4, 8) else plain
     return jax.shard_map(
         body, mesh=mesh, in_specs=placed, out_specs=P("grp", "rep"), check_vma=False
     )

time: 139 us -> 37.6 us (0.27)
  waiting for transfers between devices: 99.3 us -> 0 us
  Pallas kernels: 0 us -> 28.5 us
  between operations: 13.5 us -> 0.02 us
  matrix products: 8.06 us -> 0 us
  starting transfers between devices: 7.88 us -> 0 us
  other arithmetic: 3.76 us -> 0 us
  local copies, waits for them, and re-layouts: 6.11 us -> 8.66 us
    unnamed x3 -> x0, waiting for transfers between devices: 63.2 us -> none
    reduce_scatter x1 -> x0, waiting for transfers between devices: 29 us -> none  [body(): lax.psum_scatter(lax.dot_general(grad_pre, aggregated, (((0,), (0,)), (()...]
    pallas_call x0 -> x1, Pallas kernels: none -> 28.5 us  [fused(): pl.pallas_call(kernel, out_shape=jax.ShapeDtypeStruct((lanes, width // (2...]
    dot_general x3 -> x0, matrix products: 8.06 us -> none  [the longest x1 4.06 us: body(): lax.dot_general(grad_pre, aggregated, (((0,), (0,)), ((), ())), preferred...]
    all_to_all x2 -> x0, starting transfers between devices: 7.8 us -> none  [the longest x1 4.34 us: body(): lax.all_to_all(fetch_row, 'grp', split_axis=0, concat_axis=0, tiled=True)]
    all_to_all x2 -> x0, waiting for transfers between devices: 7.09 us -> none  [the longest x1 5.68 us: body(): lax.all_to_all(table_rows, 'grp', split_axis=0, concat_axis=0, tiled=True)]
    unnamed x11 -> x22, local copies, waits for them, and re-layouts: 1.95 us -> 7.95 us
    gather x2 -> x0, local copies, waits for them, and re-layouts: 3.28 us -> none  [the longest x1 2.63 us: body(): jnp.take(features, asked.reshape(-1), axis=0)]
  transfers between devices with their start and end apart: 4 -> 0, of which waited for: 4 -> 0; matrix products, arithmetic and copies ran while one was open for 3% -> 0% of each run, Pallas kernels for 0% -> 0%
where the time goes in v1:
time: 37.6 us; the launch traced here: 37.2 us
  Pallas kernels  28.5 us (76%)
  local copies, waits for them, and re-layouts  8.66 us (23%)
    pallas_call x1, Pallas kernels, fused(): pl.pallas_call(kernel, out_shape=jax.ShapeDtypeStruct((lanes, width // (2...  28.5 us
    unnamed x22, local copies, waits for them, and re-layouts  7.95 us

profile of v1, /device:TPU:0, one launch (start us, length us, event | category | flops | bytes accessed | tf_op | source)
XLA Modules:
  0.0 37.2 jit_solution(8410408523845751501)
XLA Ops:
  0.0 0.0 copy-start.9
  0.0 0.0 copy-start.8
  0.0 0.7 %copy-done.9 = s32[4,1]{0,1:T(1,128)S(1)} copy-done((s32[4,1]{0,1:T(1,128)S(1)}, s32[4,1]{0,1:T(1,128)}, u32[]{:S(2)}) %copy-start.9) | copy-done | bytes 40
  0.7 0.0 copy-start.7
  0.7 0.1 copy.11.live_hbm
  0.8 0.0 copy-done.8
  0.8 0.0 copy-start.6
  0.8 0.1 copy.12.block_hbm
  0.8 0.5 %copy-done.7 = f32[512]{0:T(512)S(1)} copy-done((f32[512]{0:T(512)S(1)}, f32[512]{0:T(512)}, u32[]{:S(2)}) %copy-start.7) | copy-done | bytes 2072
  1.3 0.1 copy-done.6
  1.4 0.0 copy-start
  1.4 1.1 %copy-done = bf16[512,768]{1,0:T(8,128)(2,1)S(1)} copy-done((bf16[512,768]{1,0:T(8,128)(2,1)S(1)}, bf16[512,768]{1,0:T(8,128)(2,1)}, u32[]{:S(2)}) %copy-start) | copy-done | bytes 786456
  2.6 0.0 copy-start.1
  2.6 1.1 %copy-done.1 = bf16[512,768]{1,0:T(8,128)(2,1)S(1)} copy-done((bf16[512,768]{1,0:T(8,128)(2,1)S(1)}, bf16[512,768]{1,0:T(8,128)(2,1)}, u32[]{:S(2)}) %copy-start.1) | copy-done | bytes 786456
  3.7 0.0 copy-start.2
  3.7 1.1 %copy-done.2 = bf16[768,512]{1,0:T(8,128)(2,1)S(1)} copy-done((bf16[768,512]{1,0:T(8,128)(2,1)S(1)}, bf16[768,512]{1,0:T(8,128)(2,1)}, u32[]{:S(2)}) %copy-start.2) | copy-done | bytes 786456
  4.8 0.0 copy-start.3
  4.8 1.1 %copy-done.3 = bf16[768,512]{1,0:T(8,128)(2,1)S(1)} copy-done((bf16[768,512]{1,0:T(8,128)(2,1)S(1)}, bf16[768,512]{1,0:T(8,128)(2,1)}, u32[]{:S(2)}) %copy-start.3) | copy-done | bytes 786456
  6.0 0.0 copy-start.4
  6.0 1.0 %copy-done.4 = bf16[512,512]{1,0:T(8,128)(2,1)S(1)} copy-done((bf16[512,512]{1,0:T(8,128)(2,1)S(1)}, bf16[512,512]{1,0:T(8,128)(2,1)}, u32[]{:S(2)}) %copy-start.4) | copy-done | bytes 524312
  7.0 0.0 copy-start.5
  7.0 0.9 %copy-done.5 = bf16[4,2,128,128]{3,2,1,0:T(8,128)(2,1)S(1)} copy-done((bf16[4,2,128,128]{3,2,1,0:T(8,128)(2,1)S(1)}, bf16[4,2,128,128]{3,2,1,0:T(8,128)(2,1)}, u32[]{:S(2)}) %copy-start.5) | copy-done | bytes 262168
  8.0 28.5 %sage_step.1 = f32[128,96]{1,0:T(8,128)S(1)} custom-call(bf16[512,768]{1,0:T(8,128)(2,1)S(1)} %copy-done, s32[4,64]{1,0:T(4,128)S(1)} %copy-done.6, s32[4,1]{1,0:T(4,128)S(1)} %copy.11.live_hbm, bf16[512,768]{1,0:T(8,128)(2,1)S(1)} %copy-done.1, s32[4,2]{1,0:T(4,128)S(1)} %copy.12.block_hbm, bf16[4,2,128,128]{3,2,1,0:T(8,128)(2,1)S(1)} %copy-done.5, ...), custom_call_target="tpu_custom_call" | custom-call | tf_op jit(solution)/shard_map/sage_step/pallas_call | solution.py:221
  36.5 0.7 %copy.13 = f32[128,96]{0,1:T(8,128)} copy(f32[128,96]{1,0:T(8,128)S(1)} %sage_step.1) | data formatting | bytes 98304 | tf_op jit(solution)/shard_map/sage_step/pallas_call | solution.py:221
Async XLA Ops:
  0.0 0.7 %copy-start.9 = (s32[4,1]{0,1:T(1,128)S(1)}, s32[4,1]{0,1:T(1,128)}, u32[]{:S(2)}) copy-start(s32[4,1]{0,1:T(1,128)} %param.12) | copy-start | bytes 52
  0.0 0.8 %copy-start.8 = (s32[4,2]{0,1:T(2,128)S(1)}, s32[4,2]{0,1:T(2,128)}, u32[]{:S(2)}) copy-start(s32[4,2]{0,1:T(2,128)} %param.14) | copy-start | bytes 100
  0.7 0.7 %copy-start.7 = (f32[512]{0:T(512)S(1)}, f32[512]{0:T(512)}, u32[]{:S(2)}) copy-start(f32[512]{0:T(512)} %param.18) | copy-start | bytes 6148
  0.8 0.7 %copy-start.6 = (s32[4,64]{1,0:T(4,128)S(1)}, s32[4,64]{1,0:T(4,128)}, u32[]{:S(2)}) copy-start(s32[4,64]{1,0:T(4,128)} %row_hbm.1) | copy-start | bytes 3076
  1.4 1.1 %copy-start = (bf16[512,768]{1,0:T(8,128)(2,1)S(1)}, bf16[512,768]{1,0:T(8,128)(2,1)}, u32[]{:S(2)}) copy-start(bf16[512,768]{1,0:T(8,128)(2,1)} %feat_hbm.1) | copy-start | bytes 2359300
  2.6 1.1 %copy-start.1 = (bf16[512,768]{1,0:T(8,128)(2,1)S(1)}, bf16[512,768]{1,0:T(8,128)(2,1)}, u32[]{:S(2)}) copy-start(bf16[512,768]{1,0:T(8,128)(2,1)} %seed_hbm.1) | copy-start | bytes 2359300
  3.7 1.1 %copy-start.2 = (bf16[768,512]{1,0:T(8,128)(2,1)S(1)}, bf16[768,512]{1,0:T(8,128)(2,1)}, u32[]{:S(2)}) copy-start(bf16[768,512]{1,0:T(8,128)(2,1)} %self_hbm.1) | copy-start | bytes 2359300
  4.8 1.1 %copy-start.3 = (bf16[768,512]{1,0:T(8,128)(2,1)S(1)}, bf16[768,512]{1,0:T(8,128)(2,1)}, u32[]{:S(2)}) copy-start(bf16[768,512]{1,0:T(8,128)(2,1)} %neigh_hbm.1) | copy-start | bytes 2359300
  6.0 1.0 %copy-start.4 = (bf16[512,512]{1,0:T(8,128)(2,1)S(1)}, bf16[512,512]{1,0:T(8,128)(2,1)}, u32[]{:S(2)}) copy-start(bf16[512,512]{1,0:T(8,128)(2,1)} %cot_hbm.1) | copy-start | bytes 1572868
  7.0 0.9 %copy-start.5 = (bf16[4,2,128,128]{3,2,1,0:T(8,128)(2,1)S(1)}, bf16[4,2,128,128]{3,2,1,0:T(8,128)(2,1)}, u32[]{:S(2)}) copy-start(bf16[4,2,128,128]{3,2,1,0:T(8,128)(2,1)} %tile_hbm.1) | copy-start | bytes 786436

commit v2 on v0

--- a/solution.py
+++ b/solution.py
@@ -1,10 +1,278 @@
+import functools
+
 import jax
 import jax.numpy as jnp
 from jax import lax
+from jax.experimental import pallas as pl
+from jax.experimental.pallas import tpu as pltpu
 from jax.sharding import PartitionSpec as P
 
-
-def body(
+MESH = pl.DeviceIdType.MESH
+BF16 = jnp.bfloat16
+F32 = jnp.float32
+
+
+def dot(a, b, ca=1, cb=0):
+    return lax.dot_general(a, b, (((ca,), (cb,)), ((), ())), preferred_element_type=F32)
+
+
+def kernel(
+    feat_hbm, row_hbm, live_hbm, seed_hbm, block_hbm, tile_hbm, self_hbm, neigh_hbm, bias_hbm, cot_hbm,
+    out_ref,
+    feat, row, live, seeds, block, tile, w_self, w_neigh, bias, cot,
+    request, asked, table_rows, fetched, mixed, hidden, agg_t,
+    send_c, recv_c, own, send_1, recv_1, send_2, recv_2, send_3, recv_3,
+    load_sem, ask_send, ask_recv, row_send, row_recv,
+    c_send, c_recv, s1_send, s1_recv, s2_send, s2_recv, s3_send, s3_recv,
+):
+    g, r = lax.axis_index("grp"), lax.axis_index("rep")
+    x, c = g // 2, g % 2
+    z, y = r // 2, r % 2
+    n_z = recv_3.shape[0] + 1
+    slots = row.shape[1]
+    lanes, part = own.shape[-1], own.shape[-2]
+    n_f, width_f = fetched.shape[0], fetched.shape[3]
+    sib, x_near, x_far = x * 2 + (1 - c), (1 - x) * 2 + c, (1 - x) * 2 + (1 - c)
+    group = (x_near, x_far, sib)
+    y_near = z * 2 + (1 - y)
+
+    def at(grp, rep):
+        return {"grp": grp, "rep": rep}
+
+    barrier = pltpu.get_barrier_semaphore()
+    for peer in group:
+        pl.semaphore_signal(barrier, inc=1, device_id=at(peer, r), device_id_type=MESH)
+    pl.semaphore_signal(barrier, inc=1, device_id=at(g, y_near), device_id_type=MESH)
+    for d in range(1, n_z):
+        pl.semaphore_signal(barrier, inc=1, device_id=at(g, (z + d) % n_z * 2 + y), device_id_type=MESH)
+
+    loads = {}
+
+    def load(name, src, dst):
+        copy = pltpu.make_async_copy(src, dst, load_sem.at[sum(len(v) for v in loads.values())])
+        copy.start()
+        loads.setdefault(name, []).append(copy)
+
+    def ready(*names):
+        for name in names:
+            for copy in loads[name]:
+                copy.wait()
+
+    hidden_order = (x_far, sib, x_near, g)
+
+    def load_hidden(name, src, dst):
+        for k, unit in enumerate(hidden_order):
+            cols = pl.ds(pl.multiple_of(unit * lanes, lanes), lanes)
+            load(name, src.at[:, cols], dst.at[:, k * lanes : (k + 1) * lanes])
+
+    load("ask", row_hbm, row)
+    load("ask", live_hbm, live)
+    load("feat", feat_hbm, feat)
+    load("seeds", seed_hbm, seeds)
+    load_hidden("self", self_hbm, w_self)
+    load("tile", block_hbm, block)
+    load("tile", tile_hbm, tile)
+    load_hidden("bias", bias_hbm, bias)
+    load_hidden("neigh", neigh_hbm, w_neigh)
+    load_hidden("cot", cot_hbm, cot)
+
+    ready("ask")
+    slot_ix = lax.broadcasted_iota(jnp.int32, (1, slots), 1)
+    for p in range(4):
+        line = jnp.where(slot_ix < live[0:1, p : p + 1], row[p : p + 1, :], -1)
+        line = jnp.broadcast_to(line, (8, slots))
+        request[p, :, 0:slots] = line
+        request[p, :, slots : 2 * slots] = line
+    pl.semaphore_wait(barrier, 3 + n_z)
+
+    asks = []
+    for k, peer in enumerate(group):
+        copy = pltpu.make_async_remote_copy(
+            src_ref=request.at[peer], dst_ref=asked.at[g], send_sem=ask_send.at[k], recv_sem=ask_recv.at[k],
+            device_id=at(peer, r), device_id_type=MESH,
+        )
+        copy.start()
+        asks.append(copy)
+    asked[g] = request[g]
+    ready("feat")
+
+    def picks(chip):
+        lane = lax.broadcasted_iota(jnp.int32, (1, 2 * slots), 1)
+        ix = jnp.where(lane < slots, asked[2 * chip][0:1, :], asked[2 * chip + 1][0:1, :])
+        rows_ix = lax.broadcasted_iota(jnp.int32, (feat.shape[0], 2 * slots), 0)
+        return jnp.where(rows_ix == ix, 1.0, 0.0).astype(BF16).T
+
+    def gather(pick, chip, f):
+        rows = dot(pick, feat[:, f * width_f : (f + 1) * width_f]).astype(BF16)
+        table_rows[f, 2 * chip] = rows[0:slots]
+        table_rows[f, 2 * chip + 1] = rows[slots : 2 * slots]
+
+    rows_out = {}
+
+    def send_rows(k, f):
+        copy = pltpu.make_async_remote_copy(
+            src_ref=table_rows.at[f, group[k]], dst_ref=fetched.at[f, g], send_sem=row_send.at[f, k],
+            recv_sem=row_recv.at[f, k], device_id=at(group[k], r), device_id_type=MESH,
+        )
+        copy.start()
+        rows_out[f, k] = copy
+
+    asks[0].wait()
+    asks[1].wait()
+    pick = picks(1 - x)
+    for f in range(n_f):
+        gather(pick, 1 - x, f)
+        send_rows(0, f)
+        send_rows(1, f)
+    asks[2].wait()
+    pick = picks(x)
+    for f in range(n_f):
+        gather(pick, x, f)
+        send_rows(2, f)
+        fetched[f, g] = table_rows[f, g]
+
+    ready("seeds", "self")
+    hidden[...] = dot(seeds[...], w_self[...])
+    ready("tile")
+    n_b, n_k, rows_b, cols_b = tile.shape
+    order = block[...]
+    for b in range(n_b):
+        for j in range(n_k):
+            total = jnp.zeros((rows_b, cols_b), F32)
+            for k in range(n_k):
+                here = jnp.broadcast_to(order[k : k + 1, b : b + 1], (rows_b, cols_b)) == j
+                total = jnp.where(here, tile[b, k].astype(F32), total)
+            mixed[b * rows_b : (b + 1) * rows_b, j * cols_b : (j + 1) * cols_b] = total.astype(BF16)
+    ready("bias", "neigh", "cot")
+    hidden[...] += bias[...]
+
+    for f in range(n_f):
+        for k in range(3):
+            rows_out[f, k].wait()
+        cols = slice(f * width_f, (f + 1) * width_f)
+        agg = dot(mixed[...], fetched[f].reshape(4 * slots, width_f)).astype(BF16)
+        if f < n_f - 1:
+            hidden[...] += dot(agg, w_neigh[cols, :])
+        agg_t[cols, :] = agg.T
+
+    def grad(side):
+        units = slice(side * 2 * lanes, (side + 1) * 2 * lanes)
+        pre = hidden[:, units] + dot(agg, w_neigh[cols, units])
+        sig = 0.5 * jnp.tanh(0.5 * pre) + 0.5
+        return (cot[:, units].astype(F32) * (sig * (1.0 + pre * (1.0 - sig)))).astype(BF16)
+
+    offsets = ((2, 1), (3, 0))
+
+    def weight_part(grad_side, q, ref, kind):
+        lhs = []
+        for d in offsets[q]:
+            for rep_y in (1 - y, y):
+                first = pl.multiple_of(((z + d) % n_z * 2 + rep_y) * 2 * part, 2 * part)
+                lhs.append(agg_t[pl.ds(first, 2 * part), :])
+        value = dot(jnp.concatenate(lhs, axis=0), grad_side)
+        for dd in range(2):
+            for ry in range(2):
+                for h in range(2):
+                    lo = ((dd * 2 + ry) * 2 + h) * part
+                    for rx in range(2):
+                        piece = value[lo : lo + part, rx * lanes : (rx + 1) * lanes].astype(kind)
+                        ref[(q, h) + ((rx, ry) if h == 0 else (ry, rx)) + (dd,)] = piece
+
+    def exchange(src, dst, sends, recvs, peer):
+        copy = pltpu.make_async_remote_copy(
+            src_ref=src, dst_ref=dst, send_sem=sends, recv_sem=recvs, device_id=peer, device_id_type=MESH
+        )
+        copy.start()
+        return copy
+
+    near = (at(x_near, r), at(g, y_near))
+    core_out, outs_1, outs_2, outs_3 = [], {}, {}, []
+    grad_side = grad(0)
+    for q in range(2):
+        weight_part(grad_side, q, send_c, BF16)
+        core_out.append(exchange(send_c.at[q], recv_c.at[q], c_send.at[q], c_recv.at[q], at(sib, r)))
+    grad_side = grad(1)
+    for q in range(2):
+        weight_part(grad_side, q, own, F32)
+        core_out[q].wait()
+        for h in range(2):
+            send_1[q, h] = (own[q, h, 0] + recv_c[q, h, 0].astype(F32)).astype(BF16)
+            outs_1[q, h] = exchange(send_1.at[q, h], recv_1.at[q, h], s1_send.at[q, h], s1_recv.at[q, h], near[h])
+    for q in range(2):
+        for h in range(2):
+            kept = own[q, h, 1] + recv_c[q, h, 1].astype(F32)
+            outs_1[q, h].wait()
+            kept = kept + recv_1[q, h].astype(F32)
+            send_2[q, h] = kept[0].astype(BF16)
+            outs_2[q, h] = exchange(send_2.at[q, h], recv_2.at[q, h], s2_send.at[q, h], s2_recv.at[q, h], near[1 - h])
+            own[q, h, 1, 1] = kept[1]
+    for q in range(2):
+        for h in range(2):
+            outs_2[q, h].wait()
+            for dd, d in enumerate(offsets[q]):
+                done = own[q, h, 1, 1, dd] + recv_2[q, h, dd].astype(F32)
+                if d > 0:
+                    send_3[d - 1, h] = done.astype(BF16)
+                else:
+                    own[q, h, 1, 1, dd] = done
+        for d in offsets[q]:
+            if d > 0:
+                to = at(g, (z + d) % n_z * 2 + y)
+                outs_3.append(exchange(send_3.at[d - 1], recv_3.at[d - 1], s3_send.at[d - 1], s3_recv.at[d - 1], to))
+    total = jnp.concatenate([own[1, h, 1, 1, 1] for h in range(2)], axis=0)
+    for copy in outs_3:
+        copy.wait()
+    for d in range(n_z - 1):
+        total = total + recv_3[d].astype(F32).reshape(total.shape)
+    out_ref[...] = total
+
+
+def fused(features, fetch_row, live_count, seed_features, tile_block, tile_weight, self_weight, neighbour_weight, layer_bias, cotangent):
+    width, hid = neighbour_weight.shape
+    seeds = seed_features.shape[0]
+    slots = fetch_row.shape[1]
+    n_z, n_f = 4, 3
+    lanes = hid // 4
+    part = width // (4 * n_z)
+    bias = layer_bias.reshape(1, hid)
+    operands = (features, fetch_row, live_count.T, seed_features, tile_block.T, tile_weight, self_weight, neighbour_weight, bias, cotangent)
+    n_b, n_k, rows_b, cols_b = tile_weight.shape
+    vmem = pltpu.VMEM
+    dma = pltpu.SemaphoreType.DMA
+    result = pl.pallas_call(
+        kernel,
+        out_shape=jax.ShapeDtypeStruct((width // (2 * n_z), lanes), F32),
+        in_specs=[pl.BlockSpec(memory_space=pltpu.HBM)] * len(operands),
+        out_specs=pl.BlockSpec(memory_space=vmem),
+        scratch_shapes=[vmem(a.shape, a.dtype) for a in operands] + [
+            vmem((4, 8, 2 * slots), jnp.int32),
+            vmem((4, 8, 2 * slots), jnp.int32),
+            vmem((n_f, 4, slots, width // n_f), BF16),
+            vmem((n_f, 4, slots, width // n_f), BF16),
+            vmem((seeds, n_k * cols_b), BF16),
+            vmem((seeds, hid), F32),
+            vmem((width, seeds), BF16),
+            vmem((2, 2, 2, 2, 2, part, lanes), BF16),
+            vmem((2, 2, 2, 2, 2, part, lanes), BF16),
+            vmem((2, 2, 2, 2, 2, part, lanes), F32),
+            vmem((2, 2, 2, 2, part, lanes), BF16),
+            vmem((2, 2, 2, 2, part, lanes), BF16),
+            vmem((2, 2, 2, part, lanes), BF16),
+            vmem((2, 2, 2, part, lanes), BF16),
+            vmem((n_z - 1, 2, part, lanes), BF16),
+            vmem((n_z - 1, 2, part, lanes), BF16),
+            dma((22,)), dma((3,)), dma((3,)), dma((n_f, 3)), dma((n_f, 3)),
+            dma((2,)), dma((2,)), dma((2, 2)), dma((2, 2)), dma((2, 2)), dma((2, 2)), dma((n_z - 1,)), dma((n_z - 1,)),
+        ],
+        compiler_params=pltpu.CompilerParams(
+            collective_id=0, has_side_effects=True, vmem_limit_bytes=56 * 1024 * 1024
+        ),
+        name="sage_step",
+    )(*operands)
+    return result.T
+
+
+def plain(
     features,
     fetch_row,
     live_count,
@@ -58,6 +326,7 @@
         P(),
         P(("grp", "rep"), None),
     )
+    body = fused if (mesh.shape["grp"], mesh.shape["rep"]) == (4, 8) else plain
     return jax.shard_map(
         body, mesh=mesh, in_specs=placed, out_specs=P("grp", "rep"), check_vma=False
     )

time: 139 us -> 29.2 us (0.21)
  waiting for transfers between devices: 99.3 us -> 0 us
  Pallas kernels: 0 us -> 27.6 us
  between operations: 13.5 us -> 0.01 us
  matrix products: 8.06 us -> 0 us
  starting transfers between devices: 7.88 us -> 0 us
  local copies, waits for them, and re-layouts: 6.11 us -> 1.42 us
  other arithmetic: 3.76 us -> 0 us
    unnamed x3 -> x0, waiting for transfers between devices: 63.2 us -> none
    reduce_scatter x1 -> x0, waiting for transfers between devices: 29 us -> none  [body(): lax.psum_scatter(lax.dot_general(grad_pre, aggregated, (((0,), (0,)), (()...]
    pallas_call x0 -> x1, Pallas kernels: none -> 27.6 us  [fused(): pl.pallas_call(kernel, out_shape=jax.ShapeDtypeStruct((width // (2 * n_z)...]
    dot_general x3 -> x0, matrix products: 8.06 us -> none  [the longest x1 4.06 us: body(): lax.dot_general(grad_pre, aggregated, (((0,), (0,)), ((), ())), preferred...]
    all_to_all x2 -> x0, starting transfers between devices: 7.8 us -> none  [the longest x1 4.34 us: body(): lax.all_to_all(fetch_row, 'grp', split_axis=0, concat_axis=0, tiled=True)]
    all_to_all x2 -> x0, waiting for transfers between devices: 7.09 us -> none  [the longest x1 5.68 us: body(): lax.all_to_all(table_rows, 'grp', split_axis=0, concat_axis=0, tiled=True)]
    gather x2 -> x0, local copies, waits for them, and re-layouts: 3.28 us -> none  [the longest x1 2.63 us: body(): jnp.take(features, asked.reshape(-1), axis=0)]
    select_n x4 -> x0, other arithmetic: 1.66 us -> none  [the longest x2 0.88 us: body(): jnp.take(features, asked.reshape(-1), axis=0)]
  transfers between devices with their start and end apart: 4 -> 0, of which waited for: 4 -> 0; matrix products, arithmetic and copies ran while one was open for 3% -> 0% of each run, Pallas kernels for 0% -> 0%
where the time goes in v2:
time: 29.2 us; the launch traced here: 29 us
  Pallas kernels  27.6 us (95%)
  local copies, waits for them, and re-layouts  1.42 us (5%)
    pallas_call x1, Pallas kernels, fused(): pl.pallas_call(kernel, out_shape=jax.ShapeDtypeStruct((width // (2 * n_z)...  27.6 us
    unnamed x1, local copies, waits for them, and re-layouts  1.42 us

profile of v2, /device:TPU:0, one launch (start us, length us, event | category | flops | bytes accessed | tf_op | source)
XLA Modules:
  0.0 29.0 jit_solution(5848230584626103931)
XLA Ops:
  0.0 27.6 %sage_step.1 = f32[96,128]{1,0:T(8,128)} custom-call(bf16[512,768]{1,0:T(8,128)(2,1)} %feat_hbm.1, s32[4,64]{1,0:T(4,128)} %row_hbm.1, s32[1,4]{1,0:T(1,128)} %bitcast.7, bf16[512,768]{1,0:T(8,128)(2,1)} %seed_hbm.1, s32[2,4]{1,0:T(2,128)} %bitcast.6, bf16[4,2,128,128]{3,2,1,0:T(8,128)(2,1)} %tile_hbm.1, bf16[768,512]{1,0:T(8,128)(2,1)} %self_hbm.1, ...), custom_call_target="tpu_custom_call" | custom-call | tf_op jit(solution)/shard_map/sage_step/pallas_call | solution.py:242
  27.6 1.4 %copy.12 = f32[128,96]{0,1:T(8,128)} copy(f32[128,96]{0,1:T(8,128)} %bitcast.4) | data formatting | bytes 98304

commit v3 on v2

--- a/solution.py
+++ b/solution.py
@@ -68,13 +68,6 @@
     load("ask", row_hbm, row)
     load("ask", live_hbm, live)
     load("feat", feat_hbm, feat)
-    load("seeds", seed_hbm, seeds)
-    load_hidden("self", self_hbm, w_self)
-    load("tile", block_hbm, block)
-    load("tile", tile_hbm, tile)
-    load_hidden("bias", bias_hbm, bias)
-    load_hidden("neigh", neigh_hbm, w_neigh)
-    load_hidden("cot", cot_hbm, cot)
 
     ready("ask")
     slot_ix = lax.broadcasted_iota(jnp.int32, (1, slots), 1)
@@ -94,6 +87,13 @@
         copy.start()
         asks.append(copy)
     asked[g] = request[g]
+    load("seeds", seed_hbm, seeds)
+    load_hidden("self", self_hbm, w_self)
+    load("tile", block_hbm, block)
+    load("tile", tile_hbm, tile)
+    load_hidden("bias", bias_hbm, bias)
+    load_hidden("neigh", neigh_hbm, w_neigh)
+    load_hidden("cot", cot_hbm, cot)
     ready("feat")
 
     def picks(chip):
@@ -265,7 +265,7 @@
             dma((2,)), dma((2,)), dma((2, 2)), dma((2, 2)), dma((2, 2)), dma((2, 2)), dma((n_z - 1,)), dma((n_z - 1,)),
         ],
         compiler_params=pltpu.CompilerParams(
-            collective_id=0, has_side_effects=True, vmem_limit_bytes=56 * 1024 * 1024
+            collective_id=0, has_side_effects=True, vmem_limit_bytes=24 * 1024 * 1024
         ),
         name="sage_step",
     )(*operands)

time: 29.2 us -> 35.2 us (1.21)
  local copies, waits for them, and re-layouts: 1.42 us -> 7.85 us
  Pallas kernels: 27.6 us -> 26.9 us
    unnamed x1 -> x21, local copies, waits for them, and re-layouts: 1.42 us -> 7.85 us
    pallas_call x1, Pallas kernels: 27.6 us -> 26.9 us  [fused(): pl.pallas_call(kernel, out_shape=jax.ShapeDtypeStruct((width // (2 * n_z)...]
where the time goes in v3:
time: 35.2 us; the launch traced here: 34.8 us
  Pallas kernels  26.9 us (76%)
  local copies, waits for them, and re-layouts  7.85 us (22%)
    pallas_call x1, Pallas kernels, fused(): pl.pallas_call(kernel, out_shape=jax.ShapeDtypeStruct((width // (2 * n_z)...  26.9 us
    unnamed x21, local copies, waits for them, and re-layouts  7.85 us

profile of v3, /device:TPU:0, one launch (start us, length us, event | category | flops | bytes accessed | tf_op | source)
XLA Modules:
  0.0 34.8 jit_solution(5731416686070227806)
XLA Ops:
  0.0 0.0 copy-start.7
  0.0 0.0 copy-start.6
  0.0 0.0 copy-start.8
  0.0 0.0 copy-start.9
  0.0 0.7 %copy-done.7 = f32[512]{0:T(512)S(1)} copy-done((f32[512]{0:T(512)S(1)}, f32[512]{0:T(512)}, u32[]{:S(2)}) %copy-start.7) | copy-done | bytes 2072
  0.7 0.0 copy-done.6
  0.7 0.0 copy-done.8
  0.7 0.0 copy-done.9
  0.7 0.0 copy-start
  0.7 1.1 %copy-done = bf16[512,768]{1,0:T(8,128)(2,1)S(1)} copy-done((bf16[512,768]{1,0:T(8,128)(2,1)S(1)}, bf16[512,768]{1,0:T(8,128)(2,1)}, u32[]{:S(2)}) %copy-start) | copy-done | bytes 786456
  1.8 0.0 copy-start.1
  1.9 1.1 %copy-done.1 = bf16[512,768]{1,0:T(8,128)(2,1)S(1)} copy-done((bf16[512,768]{1,0:T(8,128)(2,1)S(1)}, bf16[512,768]{1,0:T(8,128)(2,1)}, u32[]{:S(2)}) %copy-start.1) | copy-done | bytes 786456
  3.0 0.0 copy-start.2
  3.0 1.1 %copy-done.2 = bf16[768,512]{1,0:T(8,128)(2,1)S(1)} copy-done((bf16[768,512]{1,0:T(8,128)(2,1)S(1)}, bf16[768,512]{1,0:T(8,128)(2,1)}, u32[]{:S(2)}) %copy-start.2) | copy-done | bytes 786456
  4.1 0.0 copy-start.3
  4.1 1.1 %copy-done.3 = bf16[768,512]{1,0:T(8,128)(2,1)S(1)} copy-done((bf16[768,512]{1,0:T(8,128)(2,1)S(1)}, bf16[768,512]{1,0:T(8,128)(2,1)}, u32[]{:S(2)}) %copy-start.3) | copy-done | bytes 786456
  5.2 0.0 copy-start.4
  5.3 1.0 %copy-done.4 = bf16[512,512]{1,0:T(8,128)(2,1)S(1)} copy-done((bf16[512,512]{1,0:T(8,128)(2,1)S(1)}, bf16[512,512]{1,0:T(8,128)(2,1)}, u32[]{:S(2)}) %copy-start.4) | copy-done | bytes 524312
  6.3 0.0 copy-start.5
  6.3 0.9 %copy-done.5 = bf16[4,2,128,128]{3,2,1,0:T(8,128)(2,1)S(1)} copy-done((bf16[4,2,128,128]{3,2,1,0:T(8,128)(2,1)S(1)}, bf16[4,2,128,128]{3,2,1,0:T(8,128)(2,1)}, u32[]{:S(2)}) %copy-start.5) | copy-done | bytes 262168
  7.2 26.9 %sage_step.1 = f32[96,128]{1,0:T(8,128)S(1)} custom-call(bf16[512,768]{1,0:T(8,128)(2,1)S(1)} %copy-done, s32[4,64]{1,0:T(4,128)S(1)} %copy-done.6, s32[1,4]{1,0:T(1,128)S(1)} %bitcast.7, bf16[512,768]{1,0:T(8,128)(2,1)S(1)} %copy-done.1, s32[2,4]{1,0:T(2,128)S(1)} %bitcast.6, bf16[4,2,128,128]{3,2,1,0:T(8,128)(2,1)S(1)} %copy-done.5, ...), custom_call_target="tpu_custom_call" | custom-call | tf_op jit(solution)/shard_map/sage_step/pallas_call | solution.py:242
  34.2 0.6 %copy.12 = f32[128,96]{0,1:T(8,128)} copy(f32[128,96]{0,1:T(8,128)S(1)} %bitcast.4) | data formatting | bytes 98304
Async XLA Ops:
  0.0 0.7 %copy-start.7 = (f32[512]{0:T(512)S(1)}, f32[512]{0:T(512)}, u32[]{:S(2)}) copy-start(f32[512]{0:T(512)} %param.18) | copy-start | bytes 6148
  0.0 0.7 %copy-start.6 = (s32[4,64]{1,0:T(4,128)S(1)}, s32[4,64]{1,0:T(4,128)}, u32[]{:S(2)}) copy-start(s32[4,64]{1,0:T(4,128)} %row_hbm.1) | copy-start | bytes 3076
  0.0 0.7 %copy-start.8 = (s32[4,2]{0,1:T(2,128)S(1)}, s32[4,2]{0,1:T(2,128)}, u32[]{:S(2)}) copy-start(s32[4,2]{0,1:T(2,128)} %param.14) | copy-start | bytes 100
  0.0 0.7 %copy-start.9 = (s32[4,1]{0,1:T(1,128)S(1)}, s32[4,1]{0,1:T(1,128)}, u32[]{:S(2)}) copy-start(s32[4,1]{0,1:T(1,128)} %param.12) | copy-start | bytes 52
  0.7 1.1 %copy-start = (bf16[512,768]{1,0:T(8,128)(2,1)S(1)}, bf16[512,768]{1,0:T(8,128)(2,1)}, u32[]{:S(2)}) copy-start(bf16[512,768]{1,0:T(8,128)(2,1)} %feat_hbm.1) | copy-start | bytes 2359300
  1.8 1.1 %copy-start.1 = (bf16[512,768]{1,0:T(8,128)(2,1)S(1)}, bf16[512,768]{1,0:T(8,128)(2,1)}, u32[]{:S(2)}) copy-start(bf16[512,768]{1,0:T(8,128)(2,1)} %seed_hbm.1) | copy-start | bytes 2359300
  3.0 1.1 %copy-start.2 = (bf16[768,512]{1,0:T(8,128)(2,1)S(1)}, bf16[768,512]{1,0:T(8,128)(2,1)}, u32[]{:S(2)}) copy-start(bf16[768,512]{1,0:T(8,128)(2,1)} %self_hbm.1) | copy-start | bytes 2359300
  4.1 1.1 %copy-start.3 = (bf16[768,512]{1,0:T(8,128)(2,1)S(1)}, bf16[768,512]{1,0:T(8,128)(2,1)}, u32[]{:S(2)}) copy-start(bf16[768,512]{1,0:T(8,128)(2,1)} %neigh_hbm.1) | copy-start | bytes 2359300
  5.2 1.0 %copy-start.4 = (bf16[512,512]{1,0:T(8,128)(2,1)S(1)}, bf16[512,512]{1,0:T(8,128)(2,1)}, u32[]{:S(2)}) copy-start(bf16[512,512]{1,0:T(8,128)(2,1)} %cot_hbm.1) | copy-start | bytes 1572868
  6.3 0.9 %copy-start.5 = (bf16[4,2,128,128]{3,2,1,0:T(8,128)(2,1)S(1)}, bf16[4,2,128,128]{3,2,1,0:T(8,128)(2,1)}, u32[]{:S(2)}) copy-start(bf16[4,2,128,128]{3,2,1,0:T(8,128)(2,1)} %tile_hbm.1) | copy-start | bytes 786436

commit v4 on v3

--- a/solution.py
+++ b/solution.py
@@ -117,14 +117,14 @@
         copy.start()
         rows_out[f, k] = copy
 
-    asks[0].wait()
-    asks[1].wait()
+    asks[0].wait_recv()
+    asks[1].wait_recv()
     pick = picks(1 - x)
     for f in range(n_f):
         gather(pick, 1 - x, f)
         send_rows(0, f)
         send_rows(1, f)
-    asks[2].wait()
+    asks[2].wait_recv()
     pick = picks(x)
     for f in range(n_f):
         gather(pick, x, f)
@@ -148,7 +148,7 @@
 
     for f in range(n_f):
         for k in range(3):
-            rows_out[f, k].wait()
+            rows_out[f, k].wait_recv()
         cols = slice(f * width_f, (f + 1) * width_f)
         agg = dot(mixed[...], fetched[f].reshape(4 * slots, width_f)).astype(BF16)
         if f < n_f - 1:
@@ -194,21 +194,21 @@
     grad_side = grad(1)
     for q in range(2):
         weight_part(grad_side, q, own, F32)
-        core_out[q].wait()
+        core_out[q].wait_recv()
         for h in range(2):
             send_1[q, h] = (own[q, h, 0] + recv_c[q, h, 0].astype(F32)).astype(BF16)
             outs_1[q, h] = exchange(send_1.at[q, h], recv_1.at[q, h], s1_send.at[q, h], s1_recv.at[q, h], near[h])
     for q in range(2):
         for h in range(2):
             kept = own[q, h, 1] + recv_c[q, h, 1].astype(F32)
-            outs_1[q, h].wait()
+            outs_1[q, h].wait_recv()
             kept = kept + recv_1[q, h].astype(F32)
             send_2[q, h] = kept[0].astype(BF16)
             outs_2[q, h] = exchange(send_2.at[q, h], recv_2.at[q, h], s2_send.at[q, h], s2_recv.at[q, h], near[1 - h])
             own[q, h, 1, 1] = kept[1]
     for q in range(2):
         for h in range(2):
-            outs_2[q, h].wait()
+            outs_2[q, h].wait_recv()
             for dd, d in enumerate(offsets[q]):
                 done = own[q, h, 1, 1, dd] + recv_2[q, h, dd].astype(F32)
                 if d > 0:
@@ -221,10 +221,13 @@
                 outs_3.append(exchange(send_3.at[d - 1], recv_3.at[d - 1], s3_send.at[d - 1], s3_recv.at[d - 1], to))
     total = jnp.concatenate([own[1, h, 1, 1, 1] for h in range(2)], axis=0)
     for copy in outs_3:
-        copy.wait()
+        copy.wait_recv()
     for d in range(n_z - 1):
         total = total + recv_3[d].astype(F32).reshape(total.shape)
     out_ref[...] = total
+    for copies in (asks, rows_out.values(), core_out, outs_1.values(), outs_2.values(), outs_3):
+        for copy in copies:
+            copy.wait_send()
 
 
 def fused(features, fetch_row, live_count, seed_features, tile_block, tile_weight, self_weight, neighbour_weight, layer_bias, cotangent):
@@ -241,7 +244,7 @@
     dma = pltpu.SemaphoreType.DMA
     result = pl.pallas_call(
         kernel,
-        out_shape=jax.ShapeDtypeStruct((width // (2 * n_z), lanes), F32),
+        out_shape=vmem((width // (2 * n_z), lanes), F32),
         in_specs=[pl.BlockSpec(memory_space=pltpu.HBM)] * len(operands),
         out_specs=pl.BlockSpec(memory_space=vmem),
         scratch_shapes=[vmem(a.shape, a.dtype) for a in operands] + [
@@ -265,7 +268,7 @@
             dma((2,)), dma((2,)), dma((2, 2)), dma((2, 2)), dma((2, 2)), dma((2, 2)), dma((n_z - 1,)), dma((n_z - 1,)),
         ],
         compiler_params=pltpu.CompilerParams(
-            collective_id=0, has_side_effects=True, vmem_limit_bytes=24 * 1024 * 1024
+            collective_id=0, has_side_effects=True, vmem_limit_bytes=56 * 1024 * 1024
         ),
         name="sage_step",
     )(*operands)

time: 35.2 us -> 27.8 us (0.79)
  local copies, waits for them, and re-layouts: 7.85 us -> 0.62 us
    unnamed x21 -> x1, local copies, waits for them, and re-layouts: 7.85 us -> 0.62 us
where the time goes in v4:
time: 27.8 us; the launch traced here: 27.6 us
  Pallas kernels  27 us (97%)
  local copies, waits for them, and re-layouts  0.62 us (2%)
    pallas_call x1, Pallas kernels, fused(): pl.pallas_call(kernel, out_shape=vmem((width // (2 * n_z), lanes), F32),...  27 us
    unnamed x1, local copies, waits for them, and re-layouts  0.62 us

profile of v4, /device:TPU:0, one launch (start us, length us, event | category | flops | bytes accessed | tf_op | source)
XLA Modules:
  0.0 27.6 jit_solution(16304455350863581236)
XLA Ops:
  0.0 27.0 %sage_step.1 = f32[96,128]{1,0:T(8,128)S(1)} custom-call(bf16[512,768]{1,0:T(8,128)(2,1)} %feat_hbm.1, s32[4,64]{1,0:T(4,128)} %row_hbm.1, s32[1,4]{1,0:T(1,128)} %bitcast.7, bf16[512,768]{1,0:T(8,128)(2,1)} %seed_hbm.1, s32[2,4]{1,0:T(2,128)} %bitcast.6, bf16[4,2,128,128]{3,2,1,0:T(8,128)(2,1)} %tile_hbm.1, bf16[768,512]{1,0:T(8,128)(2,1)} %self_hbm.1, ...), custom_call_target="tpu_custom_call" | custom-call | tf_op jit(solution)/shard_map/sage_step/pallas_call | solution.py:245
  27.0 0.6 %copy.12 = f32[128,96]{0,1:T(8,128)} copy(f32[128,96]{0,1:T(8,128)S(1)} %bitcast.4) | data formatting | bytes 98304

commit v5 on v4

--- a/solution.py
+++ b/solution.py
@@ -43,6 +43,7 @@
     for peer in group:
         pl.semaphore_signal(barrier, inc=1, device_id=at(peer, r), device_id_type=MESH)
     pl.semaphore_signal(barrier, inc=1, device_id=at(g, y_near), device_id_type=MESH)
+    pl.semaphore_signal(barrier, inc=1, device_id=at(sib, y_near), device_id_type=MESH)
     for d in range(1, n_z):
         pl.semaphore_signal(barrier, inc=1, device_id=at(g, (z + d) % n_z * 2 + y), device_id_type=MESH)
 
@@ -76,7 +77,7 @@
         line = jnp.broadcast_to(line, (8, slots))
         request[p, :, 0:slots] = line
         request[p, :, slots : 2 * slots] = line
-    pl.semaphore_wait(barrier, 3 + n_z)
+    pl.semaphore_wait(barrier, 4 + n_z)
 
     asks = []
     for k, peer in enumerate(group):
@@ -176,7 +177,11 @@
                     lo = ((dd * 2 + ry) * 2 + h) * part
                     for rx in range(2):
                         piece = value[lo : lo + part, rx * lanes : (rx + 1) * lanes].astype(kind)
-                        ref[(q, h) + ((rx, ry) if h == 0 else (ry, rx)) + (dd,)] = piece
+                        first, second = (rx, ry) if h == 0 else (ry, rx)
+                        if ref is own and q == 0 and first == 0:
+                            send_1[q, h, second, dd] = piece.astype(BF16)
+                        else:
+                            ref[q, h, first, second, dd] = piece
 
     def exchange(src, dst, sends, recvs, peer):
         copy = pltpu.make_async_remote_copy(
@@ -186,21 +191,38 @@
         return copy
 
     near = (at(x_near, r), at(g, y_near))
-    core_out, outs_1, outs_2, outs_3 = [], {}, {}, []
+    far = (at(x_far, r), at(sib, y_near))
+    core_out, outs_1, outs_2, outs_3 = {}, {}, {}, []
+
+    def to_core(q, h, i, peer):
+        k = (q * 2 + h) * 2 + i
+        core_out[q, h, i] = exchange(send_c.at[q, h, i], recv_c.at[q, h, i], c_send.at[k], c_recv.at[k], peer)
+
     grad_side = grad(0)
-    for q in range(2):
-        weight_part(grad_side, q, send_c, BF16)
-        core_out.append(exchange(send_c.at[q], recv_c.at[q], c_send.at[q], c_recv.at[q], at(sib, r)))
+    weight_part(grad_side, 0, send_c, BF16)
+    for h in range(2):
+        to_core(0, h, 0, far[h])
+    weight_part(grad_side, 1, send_c, BF16)
+    for h in range(2):
+        to_core(1, h, 0, at(sib, r))
+    for h in range(2):
+        to_core(1, h, 1, at(sib, r))
+        to_core(0, h, 1, at(sib, r))
     grad_side = grad(1)
     for q in range(2):
         weight_part(grad_side, q, own, F32)
-        core_out[q].wait_recv()
         for h in range(2):
-            send_1[q, h] = (own[q, h, 0] + recv_c[q, h, 0].astype(F32)).astype(BF16)
+            if q == 1:
+                core_out[q, h, 0].wait_recv()
+                send_1[q, h] = (own[q, h, 0] + recv_c[q, h, 0].astype(F32)).astype(BF16)
             outs_1[q, h] = exchange(send_1.at[q, h], recv_1.at[q, h], s1_send.at[q, h], s1_recv.at[q, h], near[h])
     for q in range(2):
         for h in range(2):
+            core_out[q, h, 1].wait_recv()
             kept = own[q, h, 1] + recv_c[q, h, 1].astype(F32)
+            if q == 0:
+                core_out[q, h, 0].wait_recv()
+                kept = kept + recv_c[q, h, 0].astype(F32)
             outs_1[q, h].wait_recv()
             kept = kept + recv_1[q, h].astype(F32)
             send_2[q, h] = kept[0].astype(BF16)
@@ -225,7 +247,7 @@
     for d in range(n_z - 1):
         total = total + recv_3[d].astype(F32).reshape(total.shape)
     out_ref[...] = total
-    for copies in (asks, rows_out.values(), core_out, outs_1.values(), outs_2.values(), outs_3):
+    for copies in (asks, rows_out.values(), core_out.values(), outs_1.values(), outs_2.values(), outs_3):
         for copy in copies:
             copy.wait_send()
 
@@ -265,7 +287,7 @@
             vmem((n_z - 1, 2, part, lanes), BF16),
             vmem((n_z - 1, 2, part, lanes), BF16),
             dma((22,)), dma((3,)), dma((3,)), dma((n_f, 3)), dma((n_f, 3)),
-            dma((2,)), dma((2,)), dma((2, 2)), dma((2, 2)), dma((2, 2)), dma((2, 2)), dma((n_z - 1,)), dma((n_z - 1,)),
+            dma((8,)), dma((8,)), dma((2, 2)), dma((2, 2)), dma((2, 2)), dma((2, 2)), dma((n_z - 1,)), dma((n_z - 1,)),
         ],
         compiler_params=pltpu.CompilerParams(
             collective_id=0, has_side_effects=True, vmem_limit_bytes=56 * 1024 * 1024

time: 27.8 us -> 27.6 us (level)
  no operation moved by 1% of the time
where the time goes in v5:
time: 27.6 us; the launch traced here: 27.4 us
  Pallas kernels  26.8 us (97%)
  local copies, waits for them, and re-layouts  0.62 us (2%)
    pallas_call x1, Pallas kernels, fused(): pl.pallas_call(kernel, out_shape=vmem((width // (2 * n_z), lanes), F32),...  26.8 us
    unnamed x1, local copies, waits for them, and re-layouts  0.62 us

profile of v5, /device:TPU:0, one launch (start us, length us, event | category | flops | bytes accessed | tf_op | source)
XLA Modules:
  0.0 27.4 jit_solution(9712581058757521395)
XLA Ops:
  0.0 26.8 %sage_step.1 = f32[96,128]{1,0:T(8,128)S(1)} custom-call(bf16[512,768]{1,0:T(8,128)(2,1)} %feat_hbm.1, s32[4,64]{1,0:T(4,128)} %row_hbm.1, s32[1,4]{1,0:T(1,128)} %bitcast.7, bf16[512,768]{1,0:T(8,128)(2,1)} %seed_hbm.1, s32[2,4]{1,0:T(2,128)} %bitcast.6, bf16[4,2,128,128]{3,2,1,0:T(8,128)(2,1)} %tile_hbm.1, bf16[768,512]{1,0:T(8,128)(2,1)} %self_hbm.1, ...), custom_call_target="tpu_custom_call" | custom-call | tf_op jit(solution)/shard_map/sage_step/pallas_call | solution.py:267
  26.8 0.6 %copy.12 = f32[128,96]{0,1:T(8,128)} copy(f32[128,96]{0,1:T(8,128)S(1)} %bitcast.4) | data formatting | bytes 98304

commit v6 on v5

--- a/solution.py
+++ b/solution.py
@@ -10,6 +10,8 @@
 MESH = pl.DeviceIdType.MESH
 BF16 = jnp.bfloat16
 F32 = jnp.float32
+CHUNKS = ((0, 2), (2, 4))
+DIRECT = (0,)
 
 
 def dot(a, b, ca=1, cb=0):
@@ -162,26 +164,31 @@
         sig = 0.5 * jnp.tanh(0.5 * pre) + 0.5
         return (cot[:, units].astype(F32) * (sig * (1.0 + pre * (1.0 - sig)))).astype(BF16)
 
-    offsets = ((2, 1), (3, 0))
+    def z_by(m):
+        return (z, z + 1 - 2 * (z % 2), (z + 2) % n_z, n_z - 1 - z)[m]
+
+    z_order = tuple(range(n_z - 1, -1, -1))
+    bounds = CHUNKS
 
     def weight_part(grad_side, q, ref, kind):
         lhs = []
-        for d in offsets[q]:
+        for m in z_order[slice(*bounds[q])]:
             for rep_y in (1 - y, y):
-                first = pl.multiple_of(((z + d) % n_z * 2 + rep_y) * 2 * part, 2 * part)
+                first = pl.multiple_of((z_by(m) * 2 + rep_y) * 2 * part, 2 * part)
                 lhs.append(agg_t[pl.ds(first, 2 * part), :])
         value = dot(jnp.concatenate(lhs, axis=0), grad_side)
-        for dd in range(2):
+        for k in range(bounds[q][1] - bounds[q][0]):
+            at_z = bounds[q][0] + k
             for ry in range(2):
                 for h in range(2):
-                    lo = ((dd * 2 + ry) * 2 + h) * part
+                    lo = ((k * 2 + ry) * 2 + h) * part
                     for rx in range(2):
                         piece = value[lo : lo + part, rx * lanes : (rx + 1) * lanes].astype(kind)
                         first, second = (rx, ry) if h == 0 else (ry, rx)
-                        if ref is own and q == 0 and first == 0:
-                            send_1[q, h, second, dd] = piece.astype(BF16)
+                        if ref is own and q in DIRECT and first == 0:
+                            send_1[h, second, at_z] = piece.astype(BF16)
                         else:
-                            ref[q, h, first, second, dd] = piece
+                            ref[h, first, second, at_z] = piece
 
     def exchange(src, dst, sends, recvs, peer):
         copy = pltpu.make_async_remote_copy(
@@ -195,53 +202,57 @@
     core_out, outs_1, outs_2, outs_3 = {}, {}, {}, []
 
     def to_core(q, h, i, peer):
+        sl = pl.ds(bounds[q][0], bounds[q][1] - bounds[q][0])
         k = (q * 2 + h) * 2 + i
-        core_out[q, h, i] = exchange(send_c.at[q, h, i], recv_c.at[q, h, i], c_send.at[k], c_recv.at[k], peer)
-
+        core_out[q, h, i] = exchange(send_c.at[h, i, :, sl], recv_c.at[h, i, :, sl], c_send.at[k], c_recv.at[k], peer)
+
+    chunks = range(len(bounds))
     grad_side = grad(0)
-    weight_part(grad_side, 0, send_c, BF16)
-    for h in range(2):
-        to_core(0, h, 0, far[h])
-    weight_part(grad_side, 1, send_c, BF16)
-    for h in range(2):
-        to_core(1, h, 0, at(sib, r))
-    for h in range(2):
-        to_core(1, h, 1, at(sib, r))
-        to_core(0, h, 1, at(sib, r))
+    for q in chunks:
+        weight_part(grad_side, q, send_c, BF16)
+        for i in range(2):
+            for h in range(2):
+                to_core(q, h, i, far[h] if q in DIRECT and i == 0 else at(sib, r))
     grad_side = grad(1)
-    for q in range(2):
+    for q in chunks:
         weight_part(grad_side, q, own, F32)
+        zs = slice(*bounds[q])
+        sl = pl.ds(bounds[q][0], bounds[q][1] - bounds[q][0])
         for h in range(2):
-            if q == 1:
+            if q not in DIRECT:
                 core_out[q, h, 0].wait_recv()
-                send_1[q, h] = (own[q, h, 0] + recv_c[q, h, 0].astype(F32)).astype(BF16)
-            outs_1[q, h] = exchange(send_1.at[q, h], recv_1.at[q, h], s1_send.at[q, h], s1_recv.at[q, h], near[h])
-    for q in range(2):
+                send_1[h, :, zs] = (own[h, 0, :, zs] + recv_c[h, 0, :, zs].astype(F32)).astype(BF16)
+            k = q * 2 + h
+            outs_1[q, h] = exchange(send_1.at[h, :, sl], recv_1.at[h, :, sl], s1_send.at[k], s1_recv.at[k], near[h])
+    for q in chunks:
+        zs = slice(*bounds[q])
+        sl = pl.ds(bounds[q][0], bounds[q][1] - bounds[q][0])
         for h in range(2):
             core_out[q, h, 1].wait_recv()
-            kept = own[q, h, 1] + recv_c[q, h, 1].astype(F32)
-            if q == 0:
+            kept = own[h, 1, :, zs] + recv_c[h, 1, :, zs].astype(F32)
+            if q in DIRECT:
                 core_out[q, h, 0].wait_recv()
-                kept = kept + recv_c[q, h, 0].astype(F32)
+                kept = kept + recv_c[h, 0, :, zs].astype(F32)
             outs_1[q, h].wait_recv()
-            kept = kept + recv_1[q, h].astype(F32)
-            send_2[q, h] = kept[0].astype(BF16)
-            outs_2[q, h] = exchange(send_2.at[q, h], recv_2.at[q, h], s2_send.at[q, h], s2_recv.at[q, h], near[1 - h])
-            own[q, h, 1, 1] = kept[1]
-    for q in range(2):
+            kept = kept + recv_1[h, :, zs].astype(F32)
+            send_2[h, zs] = kept[0].astype(BF16)
+            k = q * 2 + h
+            outs_2[q, h] = exchange(send_2.at[h, sl], recv_2.at[h, sl], s2_send.at[k], s2_recv.at[k], near[1 - h])
+            own[h, 1, 1, zs] = kept[1]
+    for q in chunks:
         for h in range(2):
             outs_2[q, h].wait_recv()
-            for dd, d in enumerate(offsets[q]):
-                done = own[q, h, 1, 1, dd] + recv_2[q, h, dd].astype(F32)
-                if d > 0:
-                    send_3[d - 1, h] = done.astype(BF16)
+            for at_z in range(*bounds[q]):
+                done = own[h, 1, 1, at_z] + recv_2[h, at_z].astype(F32)
+                if z_order[at_z] > 0:
+                    send_3[z_order[at_z] - 1, h] = done.astype(BF16)
                 else:
-                    own[q, h, 1, 1, dd] = done
-        for d in offsets[q]:
-            if d > 0:
-                to = at(g, (z + d) % n_z * 2 + y)
-                outs_3.append(exchange(send_3.at[d - 1], recv_3.at[d - 1], s3_send.at[d - 1], s3_recv.at[d - 1], to))
-    total = jnp.concatenate([own[1, h, 1, 1, 1] for h in range(2)], axis=0)
+                    own[h, 1, 1, at_z] = done
+        for m in z_order[slice(*bounds[q])]:
+            if m > 0:
+                to = at(g, z_by(m) * 2 + y)
+                outs_3.append(exchange(send_3.at[m - 1], recv_3.at[m - 1], s3_send.at[m - 1], s3_recv.at[m - 1], to))
+    total = jnp.concatenate([own[h, 1, 1, n_z - 1] for h in range(2)], axis=0)
     for copy in outs_3:
         copy.wait_recv()
     for d in range(n_z - 1):
@@ -277,17 +288,17 @@
             vmem((seeds, n_k * cols_b), BF16),
             vmem((seeds, hid), F32),
             vmem((width, seeds), BF16),
-            vmem((2, 2, 2, 2, 2, part, lanes), BF16),
-            vmem((2, 2, 2, 2, 2, part, lanes), BF16),
-            vmem((2, 2, 2, 2, 2, part, lanes), F32),
-            vmem((2, 2, 2, 2, part, lanes), BF16),
-            vmem((2, 2, 2, 2, part, lanes), BF16),
-            vmem((2, 2, 2, part, lanes), BF16),
-            vmem((2, 2, 2, part, lanes), BF16),
+            vmem((2, 2, 2, n_z, part, lanes), BF16),
+            vmem((2, 2, 2, n_z, part, lanes), BF16),
+            vmem((2, 2, 2, n_z, part, lanes), F32),
+            vmem((2, 2, n_z, part, lanes), BF16),
+            vmem((2, 2, n_z, part, lanes), BF16),
+            vmem((2, n_z, part, lanes), BF16),
+            vmem((2, n_z, part, lanes), BF16),
             vmem((n_z - 1, 2, part, lanes), BF16),
             vmem((n_z - 1, 2, part, lanes), BF16),
             dma((22,)), dma((3,)), dma((3,)), dma((n_f, 3)), dma((n_f, 3)),
-            dma((8,)), dma((8,)), dma((2, 2)), dma((2, 2)), dma((2, 2)), dma((2, 2)), dma((n_z - 1,)), dma((n_z - 1,)),
+            *[dma((4 * len(CHUNKS),))] * 2, *[dma((2 * len(CHUNKS),))] * 4, dma((n_z - 1,)), dma((n_z - 1,)),
         ],
         compiler_params=pltpu.CompilerParams(
             collective_id=0, has_side_effects=True, vmem_limit_bytes=56 * 1024 * 1024

time: 27.6 us -> 27.6 us (level)
  no operation moved by 1% of the time
where the time goes in v6:
time: 27.6 us; the launch traced here: 27.4 us
  Pallas kernels  26.8 us (97%)
  local copies, waits for them, and re-layouts  0.62 us (2%)
    pallas_call x1, Pallas kernels, fused(): pl.pallas_call(kernel, out_shape=vmem((width // (2 * n_z), lanes), F32),...  26.8 us
    unnamed x1, local copies, waits for them, and re-layouts  0.62 us

profile of v6, /device:TPU:0, one launch (start us, length us, event | category | flops | bytes accessed | tf_op | source)
XLA Modules:
  0.0 27.4 jit_solution(3954842359825131099)
XLA Ops:
  0.0 26.8 %sage_step.1 = f32[96,128]{1,0:T(8,128)S(1)} custom-call(bf16[512,768]{1,0:T(8,128)(2,1)} %feat_hbm.1, s32[4,64]{1,0:T(4,128)} %row_hbm.1, s32[1,4]{1,0:T(1,128)} %bitcast.7, bf16[512,768]{1,0:T(8,128)(2,1)} %seed_hbm.1, s32[2,4]{1,0:T(2,128)} %bitcast.6, bf16[4,2,128,128]{3,2,1,0:T(8,128)(2,1)} %tile_hbm.1, bf16[768,512]{1,0:T(8,128)(2,1)} %self_hbm.1, ...), custom_call_target="tpu_custom_call" | custom-call | tf_op jit(solution)/shard_map/sage_step/pallas_call | solution.py:278
  26.8 0.6 %copy.12 = f32[128,96]{0,1:T(8,128)} copy(f32[128,96]{0,1:T(8,128)S(1)} %bitcast.4) | data formatting | bytes 98304

commit v7 on v6

--- a/solution.py
+++ b/solution.py
@@ -102,8 +102,10 @@
     def picks(chip):
         lane = lax.broadcasted_iota(jnp.int32, (1, 2 * slots), 1)
         ix = jnp.where(lane < slots, asked[2 * chip][0:1, :], asked[2 * chip + 1][0:1, :])
-        rows_ix = lax.broadcasted_iota(jnp.int32, (feat.shape[0], 2 * slots), 0)
-        return jnp.where(rows_ix == ix, 1.0, 0.0).astype(BF16).T
+        column = jnp.broadcast_to(ix, (2 * slots, 2 * slots)).T
+        column = jnp.concatenate([column] * (feat.shape[0] // (2 * slots)), axis=1)
+        rows_ix = lax.broadcasted_iota(jnp.int32, (2 * slots, feat.shape[0]), 1)
+        return jnp.where(rows_ix == column, 1.0, 0.0).astype(BF16)
 
     def gather(pick, chip, f):
         rows = dot(pick, feat[:, f * width_f : (f + 1) * width_f]).astype(BF16)
@@ -201,26 +203,30 @@
     far = (at(x_far, r), at(sib, y_near))
     core_out, outs_1, outs_2, outs_3 = {}, {}, {}, []
 
-    def to_core(q, h, i, peer):
-        sl = pl.ds(bounds[q][0], bounds[q][1] - bounds[q][0])
-        k = (q * 2 + h) * 2 + i
-        core_out[q, h, i] = exchange(send_c.at[h, i, :, sl], recv_c.at[h, i, :, sl], c_send.at[k], c_recv.at[k], peer)
-
+    def to_core(q, k, peer, *part_of):
+        place = part_of + (pl.ds(bounds[q][0], bounds[q][1] - bounds[q][0]),)
+        k = q * 3 + k
+        return exchange(send_c.at[place], recv_c.at[place], c_send.at[k], c_recv.at[k], peer)
+
+    every = slice(None)
     chunks = range(len(bounds))
     grad_side = grad(0)
     for q in chunks:
         weight_part(grad_side, q, send_c, BF16)
-        for i in range(2):
-            for h in range(2):
-                to_core(q, h, i, far[h] if q in DIRECT and i == 0 else at(sib, r))
+        if q in DIRECT:
+            core_out[q] = [to_core(q, h, far[h], h, 0, every) for h in range(2)]
+            core_out[q].append(to_core(q, 2, at(sib, r), every, 1, every))
+        else:
+            core_out[q] = [to_core(q, 0, at(sib, r), every, every, every)]
     grad_side = grad(1)
     for q in chunks:
         weight_part(grad_side, q, own, F32)
         zs = slice(*bounds[q])
         sl = pl.ds(bounds[q][0], bounds[q][1] - bounds[q][0])
+        if q not in DIRECT:
+            core_out[q][0].wait_recv()
         for h in range(2):
             if q not in DIRECT:
-                core_out[q, h, 0].wait_recv()
                 send_1[h, :, zs] = (own[h, 0, :, zs] + recv_c[h, 0, :, zs].astype(F32)).astype(BF16)
             k = q * 2 + h
             outs_1[q, h] = exchange(send_1.at[h, :, sl], recv_1.at[h, :, sl], s1_send.at[k], s1_recv.at[k], near[h])
@@ -228,10 +234,11 @@
         zs = slice(*bounds[q])
         sl = pl.ds(bounds[q][0], bounds[q][1] - bounds[q][0])
         for h in range(2):
-            core_out[q, h, 1].wait_recv()
+            if q in DIRECT and h == 0:
+                core_out[q][2].wait_recv()
             kept = own[h, 1, :, zs] + recv_c[h, 1, :, zs].astype(F32)
             if q in DIRECT:
-                core_out[q, h, 0].wait_recv()
+                core_out[q][h].wait_recv()
                 kept = kept + recv_c[h, 0, :, zs].astype(F32)
             outs_1[q, h].wait_recv()
             kept = kept + recv_1[h, :, zs].astype(F32)
@@ -258,7 +265,7 @@
     for d in range(n_z - 1):
         total = total + recv_3[d].astype(F32).reshape(total.shape)
     out_ref[...] = total
-    for copies in (asks, rows_out.values(), core_out.values(), outs_1.values(), outs_2.values(), outs_3):
+    for copies in (asks, rows_out.values(), *core_out.values(), outs_1.values(), outs_2.values(), outs_3):
         for copy in copies:
             copy.wait_send()
 
@@ -298,7 +305,7 @@
             vmem((n_z - 1, 2, part, lanes), BF16),
             vmem((n_z - 1, 2, part, lanes), BF16),
             dma((22,)), dma((3,)), dma((3,)), dma((n_f, 3)), dma((n_f, 3)),
-            *[dma((4 * len(CHUNKS),))] * 2, *[dma((2 * len(CHUNKS),))] * 4, dma((n_z - 1,)), dma((n_z - 1,)),
+            *[dma((3 * len(CHUNKS),))] * 2, *[dma((2 * len(CHUNKS),))] * 4, dma((n_z - 1,)), dma((n_z - 1,)),
         ],
         compiler_params=pltpu.CompilerParams(
             collective_id=0, has_side_effects=True, vmem_limit_bytes=56 * 1024 * 1024

time: 27.6 us -> 27.6 us (level)
  no operation moved by 1% of the time
where the time goes in v7:
time: 27.6 us; the launch traced here: 27.4 us
  Pallas kernels  26.8 us (97%)
  local copies, waits for them, and re-layouts  0.62 us (2%)
    pallas_call x1, Pallas kernels, fused(): pl.pallas_call(kernel, out_shape=vmem((width // (2 * n_z), lanes), F32),...  26.8 us
    unnamed x1, local copies, waits for them, and re-layouts  0.62 us

profile of v7, /device:TPU:0, one launch (start us, length us, event | category | flops | bytes accessed | tf_op | source)
XLA Modules:
  0.0 27.4 jit_solution(11099774798602616905)
XLA Ops:
  0.0 26.8 %sage_step.1 = f32[96,128]{1,0:T(8,128)S(1)} custom-call(bf16[512,768]{1,0:T(8,128)(2,1)} %feat_hbm.1, s32[4,64]{1,0:T(4,128)} %row_hbm.1, s32[1,4]{1,0:T(1,128)} %bitcast.7, bf16[512,768]{1,0:T(8,128)(2,1)} %seed_hbm.1, s32[2,4]{1,0:T(2,128)} %bitcast.6, bf16[4,2,128,128]{3,2,1,0:T(8,128)(2,1)} %tile_hbm.1, bf16[768,512]{1,0:T(8,128)(2,1)} %self_hbm.1, ...), custom_call_target="tpu_custom_call" | custom-call | tf_op jit(solution)/shard_map/sage_step/pallas_call | solution.py:285
  26.8 0.6 %copy.12 = f32[128,96]{0,1:T(8,128)} copy(f32[128,96]{0,1:T(8,128)S(1)} %bitcast.4) | data formatting | bytes 98304

commit v8 on v7

--- a/solution.py
+++ b/solution.py
@@ -10,8 +10,8 @@
 MESH = pl.DeviceIdType.MESH
 BF16 = jnp.bfloat16
 F32 = jnp.float32
-CHUNKS = ((0, 2), (2, 4))
-DIRECT = (0,)
+CHUNKS = ((0, 1), (1, 2), (2, 4))
+DIRECT = (0, 1)
 
 
 def dot(a, b, ca=1, cb=0):
@@ -23,9 +23,9 @@
     out_ref,
     feat, row, live, seeds, block, tile, w_self, w_neigh, bias, cot,
     request, asked, table_rows, fetched, mixed, hidden, agg_t,
-    send_c, recv_c, own, send_1, recv_1, send_2, recv_2, send_3, recv_3,
+    send_c, recv_c, own, send_1, recv_1, send_2, recv_2, send_3, recv_3, send_m, recv_m,
     load_sem, ask_send, ask_recv, row_send, row_recv,
-    c_send, c_recv, s1_send, s1_recv, s2_send, s2_recv, s3_send, s3_recv,
+    c_send, c_recv, s1_send, s1_recv, s2_send, s2_recv, s3_send, s3_recv, m_send, m_recv,
 ):
     g, r = lax.axis_index("grp"), lax.axis_index("rep")
     x, c = g // 2, g % 2
@@ -48,6 +48,9 @@
     pl.semaphore_signal(barrier, inc=1, device_id=at(sib, y_near), device_id_type=MESH)
     for d in range(1, n_z):
         pl.semaphore_signal(barrier, inc=1, device_id=at(g, (z + d) % n_z * 2 + y), device_id_type=MESH)
+    z_next = z + 1 - 2 * (z % 2)
+    pl.semaphore_signal(barrier, inc=1, device_id=at(g, z_next * 2 + 1 - y), device_id_type=MESH)
+    pl.semaphore_signal(barrier, inc=1, device_id=at(x_near, z_next * 2 + y), device_id_type=MESH)
 
     loads = {}
 
@@ -79,7 +82,7 @@
         line = jnp.broadcast_to(line, (8, slots))
         request[p, :, 0:slots] = line
         request[p, :, slots : 2 * slots] = line
-    pl.semaphore_wait(barrier, 4 + n_z)
+    pl.semaphore_wait(barrier, 6 + n_z)
 
     asks = []
     for k, peer in enumerate(group):
@@ -201,7 +204,8 @@
 
     near = (at(x_near, r), at(g, y_near))
     far = (at(x_far, r), at(sib, y_near))
-    core_out, outs_1, outs_2, outs_3 = {}, {}, {}, []
+    core_out, outs_1, outs_2, outs_3, outs_m = {}, {}, {}, [], []
+    cross = (at(g, z_by(1) * 2 + 1 - y), at(x_near, z_by(1) * 2 + y))
 
     def to_core(q, k, peer, *part_of):
         place = part_of + (pl.ds(bounds[q][0], bounds[q][1] - bounds[q][0]),)
@@ -230,42 +234,64 @@
                 send_1[h, :, zs] = (own[h, 0, :, zs] + recv_c[h, 0, :, zs].astype(F32)).astype(BF16)
             k = q * 2 + h
             outs_1[q, h] = exchange(send_1.at[h, :, sl], recv_1.at[h, :, sl], s1_send.at[k], s1_recv.at[k], near[h])
-    for q in chunks:
+    def after_first(q, h):
+        zs = slice(*bounds[q])
+        kept = own[h, 1, :, zs] + recv_c[h, 1, :, zs].astype(F32)
+        if q in DIRECT:
+            core_out[q][h].wait_recv()
+            kept = kept + recv_c[h, 0, :, zs].astype(F32)
+        outs_1[q, h].wait_recv()
+        return kept + recv_1[h, :, zs].astype(F32)
+
+    def second(q):
         zs = slice(*bounds[q])
         sl = pl.ds(bounds[q][0], bounds[q][1] - bounds[q][0])
+        core_out[q][2].wait_recv()
         for h in range(2):
-            if q in DIRECT and h == 0:
-                core_out[q][2].wait_recv()
-            kept = own[h, 1, :, zs] + recv_c[h, 1, :, zs].astype(F32)
-            if q in DIRECT:
-                core_out[q][h].wait_recv()
-                kept = kept + recv_c[h, 0, :, zs].astype(F32)
-            outs_1[q, h].wait_recv()
-            kept = kept + recv_1[h, :, zs].astype(F32)
+            kept = after_first(q, h)
             send_2[h, zs] = kept[0].astype(BF16)
             k = q * 2 + h
             outs_2[q, h] = exchange(send_2.at[h, sl], recv_2.at[h, sl], s2_send.at[k], s2_recv.at[k], near[1 - h])
             own[h, 1, 1, zs] = kept[1]
-    for q in chunks:
+
+    def third(q):
         for h in range(2):
             outs_2[q, h].wait_recv()
             for at_z in range(*bounds[q]):
                 done = own[h, 1, 1, at_z] + recv_2[h, at_z].astype(F32)
-                if z_order[at_z] > 0:
-                    send_3[z_order[at_z] - 1, h] = done.astype(BF16)
-                else:
-                    own[h, 1, 1, at_z] = done
+                send_3[z_order[at_z] - 1, h] = done.astype(BF16)
         for m in z_order[slice(*bounds[q])]:
-            if m > 0:
-                to = at(g, z_by(m) * 2 + y)
-                outs_3.append(exchange(send_3.at[m - 1], recv_3.at[m - 1], s3_send.at[m - 1], s3_recv.at[m - 1], to))
+            to = at(g, z_by(m) * 2 + y)
+            outs_3.append(exchange(send_3.at[m - 1], recv_3.at[m - 1], s3_send.at[m - 1], s3_recv.at[m - 1], to))
+
+    def second_and_third(q):
+        for h in range(2):
+            kept = after_first(q, h)
+            send_m[h, 0] = kept[0, 0].astype(BF16)
+            send_m[h, 1] = kept[1, 0].astype(BF16)
+            send_m[h, 2] = kept[0, 1].astype(BF16)
+            peers = (cross[h], at(g, z_by(1) * 2 + y), near[1 - h])
+            for i in range(3):
+                k = h * 3 + i
+                outs_m.append(exchange(send_m.at[h, i], recv_m.at[h, i], m_send.at[k], m_recv.at[k], peers[i]))
+            own[h, 1, 1, n_z - 1] = kept[1, 1]
+
+    second(0)
+    second(1)
+    third(0)
+    second_and_third(2)
+    third(1)
     total = jnp.concatenate([own[h, 1, 1, n_z - 1] for h in range(2)], axis=0)
+    for copy in outs_m:
+        copy.wait_recv()
+    for i in range(3):
+        total = total + jnp.concatenate([recv_m[h, i].astype(F32) for h in range(2)], axis=0)
     for copy in outs_3:
         copy.wait_recv()
-    for d in range(n_z - 1):
+    for d in range(1, n_z - 1):
         total = total + recv_3[d].astype(F32).reshape(total.shape)
     out_ref[...] = total
-    for copies in (asks, rows_out.values(), *core_out.values(), outs_1.values(), outs_2.values(), outs_3):
+    for copies in (asks, rows_out.values(), *core_out.values(), outs_1.values(), outs_2.values(), outs_3, outs_m):
         for copy in copies:
             copy.wait_send()
 
@@ -304,8 +330,10 @@
             vmem((2, n_z, part, lanes), BF16),
             vmem((n_z - 1, 2, part, lanes), BF16),
             vmem((n_z - 1, 2, part, lanes), BF16),
+            vmem((2, 3, part, lanes), BF16),
+            vmem((2, 3, part, lanes), BF16),
             dma((22,)), dma((3,)), dma((3,)), dma((n_f, 3)), dma((n_f, 3)),
-            *[dma((3 * len(CHUNKS),))] * 2, *[dma((2 * len(CHUNKS),))] * 4, dma((n_z - 1,)), dma((n_z - 1,)),
+            *[dma((3 * len(CHUNKS),))] * 2, *[dma((2 * len(CHUNKS),))] * 4, dma((n_z - 1,)), dma((n_z - 1,)), dma((6,)), dma((6,)),
         ],
         compiler_params=pltpu.CompilerParams(
             collective_id=0, has_side_effects=True, vmem_limit_bytes=56 * 1024 * 1024

time: 27.6 us -> 27 us (0.978)
  Pallas kernels: 26.8 us -> 26.2 us
    pallas_call x1, Pallas kernels: 26.8 us -> 26.2 us  [fused(): pl.pallas_call(kernel, out_shape=vmem((width // (2 * n_z), lanes), F32),...]
where the time goes in v8:
time: 27 us; the launch traced here: 26.8 us
  Pallas kernels  26.2 us (97%)
  local copies, waits for them, and re-layouts  0.62 us (2%)
    pallas_call x1, Pallas kernels, fused(): pl.pallas_call(kernel, out_shape=vmem((width // (2 * n_z), lanes), F32),...  26.2 us
    unnamed x1, local copies, waits for them, and re-layouts  0.62 us

profile of v8, /device:TPU:0, one launch (start us, length us, event | category | flops | bytes accessed | tf_op | source)
XLA Modules:
  0.0 26.8 jit_solution(16477836153999765543)
XLA Ops:
  0.0 26.2 %sage_step.1 = f32[96,128]{1,0:T(8,128)S(1)} custom-call(bf16[512,768]{1,0:T(8,128)(2,1)} %feat_hbm.1, s32[4,64]{1,0:T(4,128)} %row_hbm.1, s32[1,4]{1,0:T(1,128)} %bitcast.7, bf16[512,768]{1,0:T(8,128)(2,1)} %seed_hbm.1, s32[2,4]{1,0:T(2,128)} %bitcast.6, bf16[4,2,128,128]{3,2,1,0:T(8,128)(2,1)} %tile_hbm.1, bf16[768,512]{1,0:T(8,128)(2,1)} %self_hbm.1, ...), custom_call_target="tpu_custom_call" | custom-call | tf_op jit(solution)/shard_map/sage_step/pallas_call | solution.py:311
  26.2 0.6 %copy.12 = f32[128,96]{0,1:T(8,128)} copy(f32[128,96]{0,1:T(8,128)S(1)} %bitcast.4) | data formatting | bytes 98304

commit v9 on v8

--- a/solution.py
+++ b/solution.py
@@ -41,6 +41,28 @@
     def at(grp, rep):
         return {"grp": grp, "rep": rep}
 
+    loads = {}
+
+    def load(name, src, dst):
+        copy = pltpu.make_async_copy(src, dst, load_sem.at[sum(len(v) for v in loads.values())])
+        copy.start()
+        loads.setdefault(name, []).append(copy)
+
+    def ready(*names):
+        for name in names:
+            for copy in loads[name]:
+                copy.wait()
+
+    hidden_order = (x_far, sib, x_near, g)
+
+    def load_hidden(name, src, dst):
+        for k, unit in enumerate(hidden_order):
+            cols = pl.ds(pl.multiple_of(unit * lanes, lanes), lanes)
+            load(name, src.at[:, cols], dst.at[:, k * lanes : (k + 1) * lanes])
+
+    load("ask", row_hbm, row)
+    load("ask", live_hbm, live)
+
     barrier = pltpu.get_barrier_semaphore()
     for peer in group:
         pl.semaphore_signal(barrier, inc=1, device_id=at(peer, r), device_id_type=MESH)
@@ -52,27 +74,6 @@
     pl.semaphore_signal(barrier, inc=1, device_id=at(g, z_next * 2 + 1 - y), device_id_type=MESH)
     pl.semaphore_signal(barrier, inc=1, device_id=at(x_near, z_next * 2 + y), device_id_type=MESH)
 
-    loads = {}
-
-    def load(name, src, dst):
-        copy = pltpu.make_async_copy(src, dst, load_sem.at[sum(len(v) for v in loads.values())])
-        copy.start()
-        loads.setdefault(name, []).append(copy)
-
-    def ready(*names):
-        for name in names:
-            for copy in loads[name]:
-                copy.wait()
-
-    hidden_order = (x_far, sib, x_near, g)
-
-    def load_hidden(name, src, dst):
-        for k, unit in enumerate(hidden_order):
-            cols = pl.ds(pl.multiple_of(unit * lanes, lanes), lanes)
-            load(name, src.at[:, cols], dst.at[:, k * lanes : (k + 1) * lanes])
-
-    load("ask", row_hbm, row)
-    load("ask", live_hbm, live)
     load("feat", feat_hbm, feat)
 
     ready("ask")
@@ -281,6 +282,9 @@
     third(0)
     second_and_third(2)
     third(1)
+    for copies in (asks, rows_out.values(), *core_out.values(), outs_1.values(), outs_2.values(), outs_3, outs_m):
+        for copy in copies:
+            copy.wait_send()
     total = jnp.concatenate([own[h, 1, 1, n_z - 1] for h in range(2)], axis=0)
     for copy in outs_m:
         copy.wait_recv()
@@ -291,9 +295,6 @@
     for d in range(1, n_z - 1):
         total = total + recv_3[d].astype(F32).reshape(total.shape)
     out_ref[...] = total
-    for copies in (asks, rows_out.values(), *core_out.values(), outs_1.values(), outs_2.values(), outs_3, outs_m):
-        for copy in copies:
-            copy.wait_send()
 
 
 def fused(features, fetch_row, live_count, seed_features, tile_block, tile_weight, self_weight, neighbour_weight, layer_bias, cotangent):

time: 27 us -> 26.9 us (level)
  no operation moved by 1% of the time
where the time goes in v9:
time: 26.9 us; the launch traced here: 26.8 us
  Pallas kernels  26.2 us (97%)
  local copies, waits for them, and re-layouts  0.62 us (2%)
    pallas_call x1, Pallas kernels, fused(): pl.pallas_call(kernel, out_shape=vmem((width // (2 * n_z), lanes), F32),...  26.2 us
    unnamed x1, local copies, waits for them, and re-layouts  0.62 us

profile of v9, /device:TPU:0, one launch (start us, length us, event | category | flops | bytes accessed | tf_op | source)
XLA Modules:
  0.0 26.8 jit_solution(1434629879832545065)
XLA Ops:
  0.0 26.2 %sage_step.1 = f32[96,128]{1,0:T(8,128)S(1)} custom-call(bf16[512,768]{1,0:T(8,128)(2,1)} %feat_hbm.1, s32[4,64]{1,0:T(4,128)} %row_hbm.1, s32[1,4]{1,0:T(1,128)} %bitcast.7, bf16[512,768]{1,0:T(8,128)(2,1)} %seed_hbm.1, s32[2,4]{1,0:T(2,128)} %bitcast.6, bf16[4,2,128,128]{3,2,1,0:T(8,128)(2,1)} %tile_hbm.1, bf16[768,512]{1,0:T(8,128)(2,1)} %self_hbm.1, ...), custom_call_target="tpu_custom_call" | custom-call | tf_op jit(solution)/shard_map/sage_step/pallas_call | solution.py:312
  26.2 0.6 %copy.12 = f32[128,96]{0,1:T(8,128)} copy(f32[128,96]{0,1:T(8,128)S(1)} %bitcast.4) | data formatting | bytes 98304

commit v10 on v9

--- a/solution.py
+++ b/solution.py
@@ -11,7 +11,7 @@
 BF16 = jnp.bfloat16
 F32 = jnp.float32
 CHUNKS = ((0, 1), (1, 2), (2, 4))
-DIRECT = (0, 1)
+DIRECT = (0,)
 
 
 def dot(a, b, ca=1, cb=0):
@@ -247,7 +247,8 @@
     def second(q):
         zs = slice(*bounds[q])
         sl = pl.ds(bounds[q][0], bounds[q][1] - bounds[q][0])
-        core_out[q][2].wait_recv()
+        if q in DIRECT:
+            core_out[q][2].wait_recv()
         for h in range(2):
             kept = after_first(q, h)
             send_2[h, zs] = kept[0].astype(BF16)

time: 26.9 us -> 27 us (level)
  no operation moved by 1% of the time
where the time goes in v10:
time: 27 us; the launch traced here: 26.9 us
  Pallas kernels  26.2 us (97%)
  local copies, waits for them, and re-layouts  0.62 us (2%)
    pallas_call x1, Pallas kernels, fused(): pl.pallas_call(kernel, out_shape=vmem((width // (2 * n_z), lanes), F32),...  26.2 us
    unnamed x1, local copies, waits for them, and re-layouts  0.62 us

profile of v10, /device:TPU:0, one launch (start us, length us, event | category | flops | bytes accessed | tf_op | source)
XLA Modules:
  0.0 26.9 jit_solution(2961733180356266381)
XLA Ops:
  0.0 26.2 %sage_step.1 = f32[96,128]{1,0:T(8,128)S(1)} custom-call(bf16[512,768]{1,0:T(8,128)(2,1)} %feat_hbm.1, s32[4,64]{1,0:T(4,128)} %row_hbm.1, s32[1,4]{1,0:T(1,128)} %bitcast.7, bf16[512,768]{1,0:T(8,128)(2,1)} %seed_hbm.1, s32[2,4]{1,0:T(2,128)} %bitcast.6, bf16[4,2,128,128]{3,2,1,0:T(8,128)(2,1)} %tile_hbm.1, bf16[768,512]{1,0:T(8,128)(2,1)} %self_hbm.1, ...), custom_call_target="tpu_custom_call" | custom-call | tf_op jit(solution)/shard_map/sage_step/pallas_call | solution.py:313
  26.2 0.6 %copy.12 = f32[128,96]{0,1:T(8,128)} copy(f32[128,96]{0,1:T(8,128)S(1)} %bitcast.4) | data formatting | bytes 98304

commit v11 on v9

--- a/solution.py
+++ b/solution.py
@@ -301,7 +301,7 @@
     width, hid = neighbour_weight.shape
     seeds = seed_features.shape[0]
     slots = fetch_row.shape[1]
-    n_z, n_f = 4, 3
+    n_z, n_f = 4, 6
     lanes = hid // 4
     part = width // (4 * n_z)
     bias = layer_bias.reshape(1, hid)

time: 26.9 us -> 27.2 us (1.011)
  no operation moved by 1% of the time
where the time goes in v11:
time: 27.2 us; the launch traced here: 27 us
  Pallas kernels  26.4 us (97%)
  local copies, waits for them, and re-layouts  0.62 us (2%)
    pallas_call x1, Pallas kernels, fused(): pl.pallas_call(kernel, out_shape=vmem((width // (2 * n_z), lanes), F32),...  26.4 us
    unnamed x1, local copies, waits for them, and re-layouts  0.62 us

profile of v11, /device:TPU:0, one launch (start us, length us, event | category | flops | bytes accessed | tf_op | source)
XLA Modules:
  0.0 27.0 jit_solution(17778062221001933697)
XLA Ops:
  0.0 26.4 %sage_step.1 = f32[96,128]{1,0:T(8,128)S(1)} custom-call(bf16[512,768]{1,0:T(8,128)(2,1)} %feat_hbm.1, s32[4,64]{1,0:T(4,128)} %row_hbm.1, s32[1,4]{1,0:T(1,128)} %bitcast.7, bf16[512,768]{1,0:T(8,128)(2,1)} %seed_hbm.1, s32[2,4]{1,0:T(2,128)} %bitcast.6, bf16[4,2,128,128]{3,2,1,0:T(8,128)(2,1)} %tile_hbm.1, bf16[768,512]{1,0:T(8,128)(2,1)} %self_hbm.1, ...), custom_call_target="tpu_custom_call" | custom-call | tf_op jit(solution)/shard_map/sage_step/pallas_call | solution.py:312
  26.4 0.6 %copy.12 = f32[128,96]{0,1:T(8,128)} copy(f32[128,96]{0,1:T(8,128)S(1)} %bitcast.4) | data formatting | bytes 98304
